TPU v7x, 32 devices: a whole 2x2x4 slice. The times are simulated.
32 devices in a mesh: groups: 2 (over y), pool: 8 (over z, x), heads: 2 (over core).
Axes of the slice: x: 2, y: 2, z: 4, core: 2. Of those that a mesh axis runs over, the one named last changes fastest.
Arguments:
- q_latent: bfloat16 [128, 65536], P(('groups', 'pool'), 'heads'), parts along dimension 0, may hold values from -100 to 100
- q_rope: bfloat16 [128, 8192], P(('groups', 'pool'), 'heads'), parts along dimension 0, may hold values from -6 to 6
- cache_latent: bfloat16 [32768, 512], P(('groups', 'pool')), parts along dimension 0, may hold values from -4 to 4
- cache_rope: bfloat16 [64, 32768], P(None, ('groups', 'pool')), parts along dimension 1, may hold values from -6 to 6
- lengths: int32 [16, 8], P(('groups', 'pool')), parts along dimension 0, may hold values from 1 to 1024, 2048 in all within a row
- tokens_b: bfloat16 [32, 3584], P(('groups', 'pool')), parts along dimension 0, may hold values from -6 to 6
- routes: int32 [32, 8], P(('groups', 'pool')), parts along dimension 0, may hold values from 0 to 15, all different within a row; in each aligned block of 2 rows (0 to 1, 2 to 3, ...) at most 2 rows name the same one
- gates: bfloat16 [32, 8], P(('groups', 'pool')), parts along dimension 0, may hold values from 0.049804688 to 0.5
- w_gate: bfloat16 [3584, 32768], P(None, ('pool', 'heads')), may hold values from -0.09375 to 0.09375
- w_up: bfloat16 [3584, 32768], P(None, ('pool', 'heads')), may hold values from -0.09375 to 0.09375
- w_down: bfloat16 [32768, 3584], P(('pool', 'heads')), may hold values from -0.125 to 0.125
Outputs:
- attended: bfloat16 [128, 65536], P(('groups', 'pool'), 'heads'), parts along dimension 0
- moe_out: bfloat16 [32, 3584], P(('groups', 'pool')), parts along dimension 0
There are 2 independent parts, one for each index of `groups`. A program takes and returns all parts, laid end to end along the dimension named above; an argument that names none is the same for every part. Nothing has to cross between parts.
Inputs may be any that keep to these rules, and one draw needn't show every extreme that they name: In each row the lengths sum to 2048 and the largest equals 1024 exactly. `routes`: each row names 8 different experts. Among the 2 rows of one pool device no expert is named by more than 2 rows, and in some pool device's rows one expert is named by exactly 2 rows.
All inputs are finite; a program needn't handle non-finite values.
Results may differ from a plain program's by a relative error of at most 0.005.
Values may be sent and summed in bfloat16 or wider, within the bound.
No kernel may reach another device: no remote copies, remote signals or barrier semaphores. Data moves between devices by JAX's collectives and lax.ppermute only.
A program may use at most 128 MiB of HBM per device.

v0:
```python
import jax
import jax.numpy as jnp
from jax import lax
from jax.sharding import PartitionSpec as P

EXPERTS = 16


score_scale = 192.0 ** (-0.5)


def attend(queries, rope_queries, latent, rope_keys, request_lengths):
    requests = request_lengths.shape[0]
    heads_here = queries.shape[0] // requests
    scores = lax.dot_general(
        queries, latent, (((1,), (1,)), ((), ())), preferred_element_type=jnp.float32
    )
    scores = (
        scores + jnp.dot(rope_queries, rope_keys, preferred_element_type=jnp.float32)
    ) * score_scale
    finish = jnp.cumsum(request_lengths)
    starts = finish - request_lengths
    position = jnp.arange(latent.shape[0], dtype=jnp.int32)
    inside = (position[None, :] >= starts[:, None]) & (position[None, :] < finish[:, None])
    inside = jnp.repeat(inside, heads_here, axis=0)
    scores = jnp.where(inside, scores, -jnp.inf)
    highest = jnp.max(scores, axis=1, keepdims=True)
    weights = jnp.exp(scores - highest)
    shares = (weights / jnp.sum(weights, axis=1, keepdims=True)).astype(jnp.bfloat16)
    return jnp.dot(shares, latent, preferred_element_type=jnp.float32).astype(jnp.bfloat16)


def expert_weights(routes, gates):
    labels = jnp.arange(EXPERTS, dtype=jnp.int32)
    chosen = (routes[:, :, None] == labels[None, None, :]).astype(jnp.float32)
    return jnp.sum(gates.astype(jnp.float32)[:, :, None] * chosen, axis=1)


def expert_block(token_rows, gate_cols, up_cols, down_rows):
    gate_pre = jnp.dot(token_rows, gate_cols, preferred_element_type=jnp.float32)
    up_pre = jnp.dot(token_rows, up_cols, preferred_element_type=jnp.float32)
    hidden = (jax.nn.silu(gate_pre) * up_pre).astype(jnp.bfloat16)
    return jnp.dot(hidden, down_rows, preferred_element_type=jnp.float32)


def local(
    q_latent,
    q_rope,
    cache_latent,
    cache_rope,
    lengths,
    tokens_b,
    routes,
    gates,
    w_gate,
    w_up,
    w_down,
):
    latent_width = cache_latent.shape[1]
    requests = lengths.shape[1]
    queries = q_latent.reshape(-1, latent_width)
    rope_queries = q_rope.reshape(queries.shape[0], cache_rope.shape[0])
    attended = attend(queries, rope_queries, cache_latent, cache_rope, lengths[0])
    attended = attended.reshape(requests, -1)
    pool_count = lax.axis_size("pool")
    head_count = lax.axis_size("heads")
    slices = pool_count * head_count // EXPERTS
    pool_index = lax.axis_index("pool")
    head_index = lax.axis_index("heads")
    labels = jnp.arange(EXPERTS, dtype=jnp.int32)
    gate_table = expert_weights(routes, gates)
    token_count, model_width = tokens_b.shape
    all_tokens, all_table = (
        lax.all_gather(tokens_b, "pool", axis=0, tiled=True),
        lax.all_gather(gate_table.astype(jnp.bfloat16), "pool", axis=0, tiled=True),
    )
    own_expert = (pool_index * head_count + head_index) // slices
    picker = (labels == own_expert).astype(jnp.bfloat16)
    row_weights = jnp.dot(all_table, picker, preferred_element_type=jnp.float32)
    weighted_terms = expert_block(all_tokens, w_gate, w_up, w_down) * row_weights[:, None]
    returned = lax.all_to_all(
        weighted_terms.reshape(pool_count, token_count, model_width),
        "pool",
        split_axis=0,
        concat_axis=0,
        tiled=True,
    )
    local_sum = jnp.sum(returned, axis=0)
    moe_out = lax.psum(local_sum, "heads").astype(jnp.bfloat16)
    return (attended, moe_out)


def solution(mesh):
    placed = (
        P(("groups", "pool"), "heads"),
        P(("groups", "pool"), "heads"),
        P(("groups", "pool"), None),
        P(None, ("groups", "pool")),
        P(("groups", "pool"), None),
        P(("groups", "pool"), None),
        P(("groups", "pool"), None),
        P(("groups", "pool"), None),
        P(None, ("pool", "heads")),
        P(None, ("pool", "heads")),
        P(("pool", "heads"), None),
    )
    return jax.shard_map(
        local,
        mesh=mesh,
        in_specs=placed,
        out_specs=(P(("groups", "pool"), "heads"), P(("groups", "pool"), None)),
        check_vma=False,
    )
```

profile of v0, /device:TPU:0, one launch (start us, length us, event | category | flops | bytes accessed | tf_op | source)
XLA Modules:
  0.0 90.2 jit_solution(2563621714194266969)
XLA Ops:
  0.6 0.0 copy-start
  0.7 32.7 %all-gather = bf16[8,2,3584]{2,1,0:T(2,128)(2,1)S(1)} all-gather(bf16[1,2,3584]{2,1,0:T(2,128)(2,1)} %bitcast.29), channel_id=1, replica_groups=mesh['groups'=2,'pool'=8,'heads'=2] {'pool'}, dimensions={0}, use_global_device_ids=true | all-gather | bytes 129024 | tf_op jit(solution)/shard_map/all_gather | solution.py:74
  33.4 0.7 convert_element_type.23
  34.1 0.8 select_reduce_fusion
  34.8 20.3 %all-gather.1 = bf16[8,2,16]{2,1,0:T(2,128)(2,1)S(1)} all-gather(bf16[1,2,16]{2,1,0:T(2,128)(2,1)S(1)} %bitcast.30), channel_id=1, replica_groups=mesh['groups'=2,'pool'=8,'heads'=2] {'pool'}, dimensions={0}, use_global_device_ids=true | all-gather | bytes 576 | tf_op jit(solution)/shard_map/all_gather | solution.py:75
  55.2 7.2 %fusion.18 = f32[16,2048]{1,0:T(8,128)S(1)} fusion(bf16[16,3584]{1,0:T(8,128)(2,1)S(1)} %reshape.60, bf16[3584,2048]{1,0:T(8,128)(2,1)} %param.19), kind=kOutput, calls=%fused_computation.30 | convolution fusion | flops 234881024 | bytes 14925824 | tf_op jit(solution)/shard_map/dot_general | solution.py:40
  62.3 0.1 convolution_bitcast_fusion
  62.5 0.0 copy-start.1
  62.5 0.0 copy-start.3
  62.5 0.0 copy-start.4
  62.5 11.5 %convolution_multiply_fusion = f32[16,3584]{1,0:T(8,128)S(1)} fusion(bf16[2048,3584]{1,0:T(8,128)(2,1)} %param.21, bf16[16,3584]{1,0:T(8,128)(2,1)S(1)} %reshape.60, bf16[3584,2048]{1,0:T(8,128)(2,1)} %param.20, f32[16,2048]{1,0:T(8,128)S(1)} %fusion.18, f32[16]{0:T(128)S(1)} %convolution_bitcast_fusion), kind=kOutput, calls=%fused_computation | convolution fusion | flops 470016000 | bytes 29835328 | tf_op jit(solution)/shard_map/dot_general | solution.py:43
  74.0 0.8 reshape.58
  74.8 3.4 %all-to-all-start = ((f32[8,2,3584]{2,1,0:T(2,128)}), f32[8,2,3584]{2,1,0:T(2,128)S(1)}, u32[]{:S(2)}, u32[]{:S(2)}) async-start(f32[8,2,3584]{2,1,0:T(2,128)} %reshape.58), calls=%async_computation | async-start | bytes 458752 | tf_op jit(solution)/shard_map/all_to_all | solution.py:81
  78.2 0.0 copy-done.1
  78.2 0.2 reshape.55
  78.4 0.0 copy-done.3
  78.4 0.2 reshape.56
  78.6 0.0 copy-done.4
  78.6 0.2 reduce-window.7
  78.8 0.0 copy-done
  78.8 0.0 copy-start.2
  78.8 1.3 %fusion.17 = f32[512,2048]{1,0:T(8,128)S(1)} fusion(bf16[512,512]{1,0:T(8,128)(2,1)S(1)} %reshape.55, bf16[2048,512]{1,0:T(8,128)(2,1)S(1)} %copy-done), kind=kOutput, calls=%fused_computation.29 | convolution fusion | flops 1073741824 | bytes 6815744 | tf_op jit(solution)/shard_map/dot_general | solution.py:15
  80.1 0.1 fusion.10
  80.2 0.0 copy-done.2
  80.2 0.9 %fusion.16 = (f32[512]{0:T(512)S(1)}, f32[512,2048]{1,0:T(8,128)S(1)}) fusion(f32[512,2048]{1,0:T(8,128)S(1)} %fusion.17, bf16[512,64]{1,0:T(8,128)(2,1)S(1)} %reshape.56, bf16[64,2048]{1,0:T(8,128)(2,1)S(1)} %copy-done.2, pred[8,2048]{1,0:T(8,128)(4,1)S(1)} %fusion.10), kind=kOutput, calls=%fused_computation.28 | convolution fusion | flops 138411520 | bytes 8734720 | tf_op jit(solution)/shard_map/dot_general | solution.py:19
  81.2 0.7 fusion
  81.9 1.4 %fusion.3 = bf16[512,512]{1,0:T(8,128)(2,1)S(1)} fusion(bf16[2048,512]{1,0:T(8,128)(2,1)S(1)} %copy-done, f32[512,2048]{1,0:T(8,128)S(1)} %get-tuple-element.3, f32[512]{0:T(512)S(1)} %fusion, f32[512]{0:T(512)S(1)} %get-tuple-element.2), kind=kOutput, calls=%fused_computation.8 | convolution fusion | flops 1077149696 | bytes 6819840 | tf_op jit(solution)/shard_map/dot_general | solution.py:30
  83.3 1.0 %reshape.57 = bf16[8,32768]{1,0:T(8,128)(2,1)} reshape(bf16[512,512]{1,0:T(8,128)(2,1)S(1)} %fusion.3) | data formatting | bytes 1048576 | tf_op jit(solution)/shard_map/reshape | solution.py:64
  84.3 1.8 %all-to-all-done = f32[8,2,3584]{2,1,0:T(2,128)S(1)} async-done(((f32[8,2,3584]{2,1,0:T(2,128)}), f32[8,2,3584]{2,1,0:T(2,128)S(1)}, u32[]{:S(2)}, u32[]{:S(2)}) %all-to-all-start) | async-done | bytes 229408 | tf_op jit(solution)/shard_map/all_to_all | solution.py:81
  86.1 0.1 reduce_sum.29
  86.2 4.0 %psum.7 = bf16[2,3584]{1,0:T(2,128)(2,1)} all-reduce(f32[2,3584]{1,0:T(2,128)S(1)} %reduce_sum.29), channel_id=1, replica_groups=mesh['groups'=2,'pool'=8,'heads'=2] {'heads'}, use_global_device_ids=true, to_apply=%region_5.6 | all-reduce | flops 7168 | bytes 43008 | tf_op jit(solution)/shard_map/psum | solution.py:89
  (2 shorter events, 0.1 us)
Async XLA Ops:
  0.6 78.2 %copy-start = (bf16[2048,512]{1,0:T(8,128)(2,1)S(1)}, bf16[2048,512]{1,0:T(8,128)(2,1)}, u32[]{:S(2)}) copy-start(bf16[2048,512]{1,0:T(8,128)(2,1)} %param.13) | copy-start | bytes 6291460
  62.5 15.7 %copy-start.1 = (bf16[8,32768]{1,0:T(8,128)(2,1)S(1)}, bf16[8,32768]{1,0:T(8,128)(2,1)}, u32[]{:S(2)}) copy-start(bf16[8,32768]{1,0:T(8,128)(2,1)} %param.11) | copy-start | bytes 1572868
  62.5 16.0 %copy-start.3 = (bf16[8,4096]{1,0:T(8,128)(2,1)S(1)}, bf16[8,4096]{1,0:T(8,128)(2,1)}, u32[]{:S(2)}) copy-start(bf16[8,4096]{1,0:T(8,128)(2,1)} %param.12) | copy-start | bytes 196612
  62.5 16.2 %copy-start.4 = (s32[1,8]{1,0:T(1,128)S(1)}, s32[1,8]{1,0:T(1,128)}, u32[]{:S(2)}) copy-start(s32[1,8]{1,0:T(1,128)} %param.15) | copy-start | bytes 100
  74.8 11.3 %all-to-all-start = ((f32[8,2,3584]{2,1,0:T(2,128)}), f32[8,2,3584]{2,1,0:T(2,128)S(1)}, u32[]{:S(2)}, u32[]{:S(2)}) async-start(f32[8,2,3584]{2,1,0:T(2,128)} %reshape.58), calls=%async_computation | async-start | bytes 458752 | tf_op jit(solution)/shard_map/all_to_all | solution.py:81
  78.8 1.4 %copy-start.2 = (bf16[64,2048]{1,0:T(8,128)(2,1)S(1)}, bf16[64,2048]{1,0:T(8,128)(2,1)}, u32[]{:S(2)}) copy-start(bf16[64,2048]{1,0:T(8,128)(2,1)} %param.14) | copy-start | bytes 786436
where the time goes:
time: 90.5 us; the launch traced here: 90.2 us
  blocking collectives  57 us (63%)
  matrix products  22.4 us (25%)
  starting transfers between devices  3.4 us (4%)
  other arithmetic  2.49 us (3%)
  local copies, waits for them, and re-layouts  2.33 us (3%)
  waiting for transfers between devices  1.82 us (2%)
    all_gather x1, blocking collectives, local(): lax.all_gather(tokens_b, 'pool', axis=0, tiled=True)  32.7 us
    all_gather x1, blocking collectives, local(): lax.all_gather(gate_table.astype(jnp.bfloat16), 'pool', axis=0, tiled=True)  20.3 us
    dot_general x1, matrix products, expert_block(): return jnp.dot(hidden, down_rows, preferred_element_type=jnp.float32)  11.5 us
    dot_general x1, matrix products, expert_block(): jnp.dot(token_rows, gate_cols, preferred_element_type=jnp.float32)  7.18 us
    psum x1, blocking collectives, local(): moe_out = lax.psum(local_sum, 'heads').astype(jnp.bfloat16)  3.99 us
    all_to_all x1, starting transfers between devices, local(): lax.all_to_all(weighted_terms.reshape(pool_count, token_count, model_widt...  3.4 us
    all_to_all x1, waiting for transfers between devices, local(): lax.all_to_all(weighted_terms.reshape(pool_count, token_count, model_widt...  1.82 us
  transfers between devices with their start and end apart: 1, of which 1 were waited for; matrix products, arithmetic and copies ran while one was open for 7% of the time, Pallas kernels for 0%

commit v1 on v0

v1 whole, which is shorter than its diff:
```python
import functools

import jax
import jax.numpy as jnp
from jax import lax
from jax.experimental import pallas as pl
from jax.experimental.pallas import tpu as pltpu
from jax.sharding import PartitionSpec as P

EXPERTS = 16
LANES = 128

score_scale = 192.0 ** (-0.5)


def attend(queries, rope_queries, latent, rope_keys, request_lengths):
    requests = request_lengths.shape[0]
    heads_here = queries.shape[0] // requests
    scores = lax.dot_general(
        queries, latent, (((1,), (1,)), ((), ())), preferred_element_type=jnp.float32
    )
    scores = (
        scores + jnp.dot(rope_queries, rope_keys, preferred_element_type=jnp.float32)
    ) * score_scale
    finish = jnp.cumsum(request_lengths)
    starts = finish - request_lengths
    position = jnp.arange(latent.shape[0], dtype=jnp.int32)
    inside = (position[None, :] >= starts[:, None]) & (position[None, :] < finish[:, None])
    inside = jnp.repeat(inside, heads_here, axis=0)
    scores = jnp.where(inside, scores, -jnp.inf)
    highest = jnp.max(scores, axis=1, keepdims=True)
    weights = jnp.exp(scores - highest)
    shares = (weights / jnp.sum(weights, axis=1, keepdims=True)).astype(jnp.bfloat16)
    return jnp.dot(shares, latent, preferred_element_type=jnp.float32).astype(jnp.bfloat16)


def expert_weights(routes, gates):
    labels = jnp.arange(LANES, dtype=jnp.int32)
    chosen = (routes[:, :, None] == labels[None, None, :]).astype(jnp.float32)
    return jnp.sum(gates.astype(jnp.float32)[:, :, None] * chosen, axis=1)


def row_step(total, most=512):
    return next(s for s in (512, 256, 128, 64, 32, 16) if s <= most and total % s == 0)


def cuts(array):
    step = row_step(array.shape[0])
    return [(k, step) for k in range(0, array.shape[0], step)]


def expert_kernel(own_ref, rows_ref, gate_ref, up_ref, down_ref, out_ref, gate_buf, up_buf, down_buf, sems):
    width = down_ref.shape[1]
    ff = gate_ref.shape[1]
    count = rows_ref.shape[0] * rows_ref.shape[1]
    copies, pending = {}, 0
    for name, source, target in (("gate", gate_ref, gate_buf), ("up", up_ref, up_buf), ("down", down_ref, down_buf)):
        copies[name] = []
        for k, step in cuts(source):
            rows = pl.ds(k, step)
            copies[name].append(pltpu.make_async_copy(source.at[rows], target.at[rows], sems.at[pending]))
            copies[name][-1].start()
            pending += 1
    packed = rows_ref[...].reshape(count, rows_ref.shape[2])
    gate_pre = jnp.zeros((count, ff), jnp.float32)
    up_pre = jnp.zeros((count, ff), jnp.float32)
    for (k, step), copy in zip(cuts(gate_ref), copies["gate"]):
        copy.wait()
        gate_pre += jnp.dot(
            packed[:, k : k + step], gate_buf[k : k + step, :], preferred_element_type=jnp.float32
        )
    for (k, step), copy in zip(cuts(up_ref), copies["up"]):
        copy.wait()
        up_pre += jnp.dot(
            packed[:, k : k + step], up_buf[k : k + step, :], preferred_element_type=jnp.float32
        )
    hidden = (gate_pre / (1.0 + jnp.exp(-gate_pre)) * up_pre).astype(jnp.bfloat16)
    table = packed[:, width:].astype(jnp.float32)
    label = lax.broadcasted_iota(jnp.int32, table.shape, 1)
    weight = jnp.sum(jnp.where(label == own_ref[0], table, 0.0), axis=1, keepdims=True)
    total = jnp.zeros((count, width), jnp.float32)
    for (k, step), copy in zip(cuts(down_ref), copies["down"]):
        copy.wait()
        total += jnp.dot(hidden[:, k : k + step], down_buf[k : k + step, :], preferred_element_type=jnp.float32)
    out_ref[...] = (total * weight).astype(jnp.bfloat16).reshape(out_ref.shape)


def local(q_latent, q_rope, cache_latent, cache_rope, lengths, tokens_b, routes, gates, w_gate, w_up, w_down):
    latent_width = cache_latent.shape[1]
    requests = lengths.shape[1]
    pool_count = lax.axis_size("pool")
    head_count = lax.axis_size("heads")
    slices = pool_count * head_count // EXPERTS
    own_expert = (lax.axis_index("pool") * head_count + lax.axis_index("heads")) // slices
    token_count, model_width = tokens_b.shape
    table = expert_weights(routes, gates).astype(jnp.bfloat16)
    packed = jnp.concatenate([tokens_b, table], axis=1)
    all_rows = lax.all_to_all(
        jnp.broadcast_to(packed[None], (pool_count,) + packed.shape), "pool", split_axis=0, concat_axis=0, tiled=True
    )
    weights = (w_gate, w_up, w_down)
    terms = pl.pallas_call(
        expert_kernel,
        out_shape=jax.ShapeDtypeStruct((pool_count, token_count, model_width), jnp.bfloat16),
        in_specs=[pl.BlockSpec(memory_space=pltpu.SMEM), pl.BlockSpec(memory_space=pltpu.VMEM)]
        + [pl.BlockSpec(memory_space=pl.ANY)] * 3,
        out_specs=pl.BlockSpec(memory_space=pltpu.VMEM),
        scratch_shapes=[pltpu.VMEM(w.shape, w.dtype) for w in weights]
        + [pltpu.SemaphoreType.DMA((sum(len(cuts(w)) for w in weights),))],
        compiler_params=pltpu.CompilerParams(vmem_limit_bytes=sum(w.size * 2 for w in weights) + (10 << 20)),
    )(
        own_expert.astype(jnp.int32)[None],
        all_rows,
        *[pltpu.with_memory_space_constraint(w, pltpu.HBM) for w in weights],
    )
    terms, q_latent, q_rope, lengths = lax.optimization_barrier((terms, q_latent, q_rope, lengths))
    returned = lax.all_to_all(terms, "pool", split_axis=0, concat_axis=0, tiled=True)
    local_sum = jnp.sum(returned.astype(jnp.float32), axis=0)
    other = lax.ppermute(local_sum, "heads", [(0, 1), (1, 0)])
    moe_out = (local_sum + other).astype(jnp.bfloat16)
    queries = q_latent.reshape(-1, latent_width)
    rope_queries = q_rope.reshape(queries.shape[0], cache_rope.shape[0])
    attended = attend(queries, rope_queries, cache_latent, cache_rope, lengths[0]).reshape(requests, -1)
    return (attended, moe_out)


def solution(mesh):
    rows = P(("groups", "pool"), None)
    split = P(("groups", "pool"), "heads")
    placed = (split, split, rows, P(None, ("groups", "pool")), rows, rows, rows, rows)
    weights = (P(None, ("pool", "heads")),) * 2 + (P(("pool", "heads"), None),)
    return jax.shard_map(
        local, mesh=mesh, in_specs=placed + weights, out_specs=(split, rows), check_vma=False
    )
```

time: 90.5 us -> 50.4 us (0.56)
  blocking collectives: 57 us -> 0 us
  matrix products: 22.4 us -> 5.72 us
  Pallas kernels: 0 us -> 15.1 us
  waiting for transfers between devices: 1.82 us -> 9.47 us
  starting transfers between devices: 3.4 us -> 10.7 us
  local copies, waits for them, and re-layouts: 2.33 us -> 4.12 us
  other arithmetic: 2.49 us -> 3.99 us
    all_gather x2 -> x0, blocking collectives: 53 us -> none  [the longest x1 32.7 us: local(): lax.all_gather(tokens_b, 'pool', axis=0, tiled=True)]
    dot_general x3 -> x0, matrix products: 18.8 us -> none  [the longest x1 11.5 us: expert_block(): return jnp.dot(hidden, down_rows, preferred_element_type=jnp.float32)]
    pallas_call x0 -> x1, Pallas kernels: none -> 15.1 us  [local(): pl.pallas_call(expert_kernel, out_shape=jax.ShapeDtypeStruct((pool_count,...]
    all_to_all x1 -> x2, waiting for transfers between devices: 1.82 us -> 9.46 us  [the longest x1 7.26 us: local(): lax.all_to_all(jnp.broadcast_to(packed[None], (pool_count,) + packed.shap...]
    all_to_all x1 -> x2, starting transfers between devices: 3.4 us -> 10.6 us  [the longest x1 7.25 us: local(): lax.all_to_all(jnp.broadcast_to(packed[None], (pool_count,) + packed.shap...]
    psum x1 -> x0, blocking collectives: 3.99 us -> none  [local(): moe_out = lax.psum(local_sum, 'heads').astype(jnp.bfloat16)]
    dot_general x1, matrix products: 1.38 us -> 3.51 us  [attend(): jnp.dot(shares, latent, preferred_element_type=jnp.float32)]
    unnamed x11 -> x12, local copies, waits for them, and re-layouts: 0.07 us -> 1.95 us
  transfers between devices with their start and end apart: 1 -> 3, of which waited for: 1 -> 2; matrix products, arithmetic and copies ran while one was open for 7% -> 15% of each run, Pallas kernels for 0% -> 0%
where the time goes in v1:
time: 50.4 us; the launch traced here: 49.8 us
  Pallas kernels  15.1 us (30%)
  starting transfers between devices  10.7 us (21%)
  waiting for transfers between devices  9.47 us (19%)
  matrix products  5.72 us (11%)
  local copies, waits for them, and re-layouts  4.12 us (8%)
  other arithmetic  3.99 us (8%)
  between operations  0.75 us (1%)
    pallas_call x1, Pallas kernels, local(): pl.pallas_call(expert_kernel, out_shape=jax.ShapeDtypeStruct((pool_count,...  15.1 us
    all_to_all x1, waiting for transfers between devices, local(): lax.all_to_all(jnp.broadcast_to(packed[None], (pool_count,) + packed.shap...  7.26 us
    all_to_all x1, starting transfers between devices, local(): lax.all_to_all(jnp.broadcast_to(packed[None], (pool_count,) + packed.shap...  7.25 us
    dot_general x1, matrix products, attend(): jnp.dot(shares, latent, preferred_element_type=jnp.float32)  3.51 us
    all_to_all x1, starting transfers between devices, local(): lax.all_to_all(terms, 'pool', split_axis=0, concat_axis=0, tiled=True)  3.37 us
    all_to_all x1, waiting for transfers between devices, local(): lax.all_to_all(terms, 'pool', split_axis=0, concat_axis=0, tiled=True)  2.2 us
    unnamed x12, local copies, waits for them, and re-layouts  1.95 us
    dot_general x1, matrix products, attend(): lax.dot_general(queries, latent, (((1,), (1,)), ((), ())), preferred_elem...  1.28 us
  transfers between devices with their start and end apart: 3, of which 2 were waited for; matrix products, arithmetic and copies ran while one was open for 15% of the time, Pallas kernels for 0%

profile of v1, /device:TPU:0, one launch (start us, length us, event | category | flops | bytes accessed | tf_op | source)
XLA Modules:
  0.0 49.8 jit_solution(10274916363242421272)
XLA Ops:
  0.6 0.0 copy-start
  0.6 0.8 %convert_element_type.19 = f32[2,8]{1,0:T(2,128)S(1)} convert(bf16[2,8]{1,0:T(2,128)(2,1)} %param.18) | non-fusion elementwise | flops 16 | bytes 96 | tf_op jit(solution)/shard_map/convert_element_type | solution.py:40
  1.5 0.8 %select_reduce_fusion = bf16[2,128]{1,0:T(2,128)(2,1)S(1)} fusion(f32[2,8]{1,0:T(2,128)S(1)} %convert_element_type.19, s32[2,8]{1,0:T(2,128)} %param.17), kind=kLoop, calls=%fused_computation.12 | loop fusion | flops 5888 | bytes 640 | tf_op jit(solution)/shard_map/reduce_sum | solution.py:40
  2.2 0.7 %pad_maximum_fusion = bf16[2,3712]{1,0:T(2,128)(2,1)S(1)} fusion(bf16[2,128]{1,0:T(2,128)(2,1)S(1)} %select_reduce_fusion, bf16[2,3584]{1,0:T(2,128)(2,1)} %param.16), kind=kLoop, calls=%fused_computation.11 | loop fusion | flops 29696 | bytes 29696 | tf_op jit(solution)/shard_map/concatenate | solution.py:97
  2.9 0.7 %broadcast_in_dim.10 = bf16[8,2,3712]{2,1,0:T(2,128)(2,1)} broadcast(bf16[2,3712]{1,0:T(2,128)(2,1)S(1)} %pad_maximum_fusion), dimensions={1,2} | broadcast | bytes 133632 | tf_op jit(solution)/shard_map/broadcast_in_dim | solution.py:99
  3.7 7.3 %all-to-all-start = ((bf16[8,2,3712]{2,1,0:T(2,128)(2,1)}), bf16[8,2,3712]{2,1,0:T(2,128)(2,1)S(1)}, u32[]{:S(2)}, u32[]{:S(2)}) async-start(bf16[8,2,3712]{2,1,0:T(2,128)(2,1)} %broadcast_in_dim.10), calls=%async_computation | async-start | bytes 237568 | tf_op jit(solution)/shard_map/all_to_all | solution.py:98
  10.9 7.3 %all-to-all-done.rows_ref = bf16[8,2,3712]{2,1,0:T(2,128)(2,1)S(1)} async-done(((bf16[8,2,3712]{2,1,0:T(2,128)(2,1)}), bf16[8,2,3712]{2,1,0:T(2,128)(2,1)S(1)}, u32[]{:S(2)}, u32[]{:S(2)}) %all-to-all-start) | async-done | bytes 118816 | tf_op jit(solution)/shard_map/all_to_all | solution.py:98
  18.2 0.0 copy-start.2
  18.2 0.0 copy-start.4
  18.2 0.0 copy-start.5
  18.2 15.1 %shard_map.122 = bf16[8,2,3584]{2,1,0:T(2,128)(2,1)} custom-call(s32[1]{0:T(128)} %bitcast.own_ref, bf16[8,2,3712]{2,1,0:T(2,128)(2,1)S(1)} %all-to-all-done.rows_ref, bf16[3584,2048]{1,0:T(8,128)(2,1)} %gate_ref.1, bf16[3584,2048]{1,0:T(8,128)(2,1)} %up_ref.1, bf16[2048,3584]{1,0:T(8,128)(2,1)} %down_ref.1), custom_call_target="tpu_custom_call" | custom-call | tf_op jit(solution)/shard_map/pallas_call | solution.py:102
  33.2 0.0 copy-done.2
  33.3 0.2 reshape.52
  33.5 0.0 copy-done.4
  33.5 0.2 reshape.53
  33.7 0.0 copy-done.5
  33.7 0.2 reduce-window.7
  33.9 3.4 %all-to-all-start.1 = ((bf16[8,2,3584]{2,1,0:T(2,128)(2,1)}), bf16[8,2,3584]{2,1,0:T(2,128)(2,1)S(1)}, u32[]{:S(2)}, u32[]{:S(2)}) async-start(bf16[8,2,3584]{2,1,0:T(2,128)(2,1)} %shard_map.122), calls=%async_computation.1 | async-start | bytes 229376 | tf_op jit(solution)/shard_map/all_to_all | solution.py:117
  37.3 0.0 copy-done
  37.3 0.0 copy-start.3
  37.3 1.3 %fusion.5 = f32[512,2048]{1,0:T(8,128)S(1)} fusion(bf16[512,512]{1,0:T(8,128)(2,1)S(1)} %reshape.52, bf16[2048,512]{1,0:T(8,128)(2,1)S(1)} %copy-done), kind=kOutput, calls=%fused_computation.16 | convolution fusion | flops 1073741824 | bytes 6815744 | tf_op jit(solution)/shard_map/dot_general | solution.py:19
  38.6 0.1 fusion.3
  38.7 0.0 copy-done.3
  38.7 0.9 %fusion.4 = (f32[512]{0:T(512)S(1)}, f32[512,2048]{1,0:T(8,128)S(1)}) fusion(f32[512,2048]{1,0:T(8,128)S(1)} %fusion.5, bf16[512,64]{1,0:T(8,128)(2,1)S(1)} %reshape.53, bf16[64,2048]{1,0:T(8,128)(2,1)S(1)} %copy-done.3, pred[8,2048]{1,0:T(8,128)(4,1)S(1)} %fusion.3), kind=kOutput, calls=%fused_computation.15 | convolution fusion | flops 138411520 | bytes 8734720 | tf_op jit(solution)/shard_map/dot_general | solution.py:23
  39.6 0.0 copy-start.1
  39.6 1.9 %copy-done.1 = f32[512,2048]{1,0:T(8,128)} copy-done((f32[512,2048]{1,0:T(8,128)}, f32[512,2048]{1,0:T(8,128)S(1)}, u32[]{:S(2)}) %copy-start.1) | copy-done | bytes 4194328
  41.5 0.7 %fusion = f32[512]{0:T(512)S(1)} fusion(f32[512,2048]{1,0:T(8,128)S(1)} %get-tuple-element.11, f32[512]{0:T(512)S(1)} %get-tuple-element.10), kind=kLoop, calls=%fused_computation.3 | loop fusion | flops 2096640 | bytes 4198400 | tf_op jit(solution)/shard_map/reduce_sum | solution.py:33
  42.2 2.2 %all-to-all-done.1 = bf16[8,2,3584]{2,1,0:T(2,128)(2,1)S(1)} async-done(((bf16[8,2,3584]{2,1,0:T(2,128)(2,1)}), bf16[8,2,3584]{2,1,0:T(2,128)(2,1)S(1)}, u32[]{:S(2)}, u32[]{:S(2)}) %all-to-all-start.1) | async-done | bytes 114720 | tf_op jit(solution)/shard_map/all_to_all | solution.py:117
  44.4 0.1 convert_reduce_fusion
  44.5 0.1 collective-permute-start
  44.6 3.5 %fusion.2 = bf16[512,512]{1,0:T(8,128)(2,1)S(1)} fusion(bf16[2048,512]{1,0:T(8,128)(2,1)S(1)} %copy-done, f32[512,2048]{1,0:T(8,128)} %copy-done.1, f32[512]{0:T(512)S(1)} %fusion, f32[512]{0:T(512)S(1)} %get-tuple-element.10), kind=kOutput, calls=%fused_computation.5 | convolution fusion | flops 1077149696 | bytes 6819840 | tf_op jit(solution)/shard_map/dot_general | solution.py:34
  48.1 1.0 %reshape.54 = bf16[8,32768]{1,0:T(8,128)(2,1)} reshape(bf16[512,512]{1,0:T(8,128)(2,1)S(1)} %fusion.2) | data formatting | bytes 1048576 | tf_op jit(solution)/shard_map/reshape | solution.py:123
  49.2 0.0 collective-permute-done
  49.2 0.6 %add_convert_fusion = bf16[2,3584]{1,0:T(2,128)(2,1)} fusion(f32[2,3584]{1,0:T(2,128)S(1)} %convert_reduce_fusion, f32[2,3584]{1,0:T(2,128)S(1)} %collective-permute-done), kind=kLoop, calls=%fused_computation.10 | loop fusion | flops 14336 | bytes 71680 | tf_op jit(solution)/shard_map/convert_element_type | solution.py:120
  (1 shorter events, 0.0 us)
Async XLA Ops:
  0.6 36.6 %copy-start = (bf16[2048,512]{1,0:T(8,128)(2,1)S(1)}, bf16[2048,512]{1,0:T(8,128)(2,1)}, u32[]{:S(2)}) copy-start(bf16[2048,512]{1,0:T(8,128)(2,1)} %param.13) | copy-start | bytes 6291460
  3.7 14.5 %all-to-all-start = ((bf16[8,2,3712]{2,1,0:T(2,128)(2,1)}), bf16[8,2,3712]{2,1,0:T(2,128)(2,1)S(1)}, u32[]{:S(2)}, u32[]{:S(2)}) async-start(bf16[8,2,3712]{2,1,0:T(2,128)(2,1)} %broadcast_in_dim.10), calls=%async_computation | async-start | bytes 237568 | tf_op jit(solution)/shard_map/all_to_all | solution.py:98
  18.2 15.1 %copy-start.2 = (bf16[8,32768]{1,0:T(8,128)(2,1)S(1)}, bf16[8,32768]{1,0:T(8,128)(2,1)}, u32[]{:S(2)}) copy-start(bf16[8,32768]{1,0:T(8,128)(2,1)} %param.11) | copy-start | bytes 1572868
  18.2 15.3 %copy-start.4 = (bf16[8,4096]{1,0:T(8,128)(2,1)S(1)}, bf16[8,4096]{1,0:T(8,128)(2,1)}, u32[]{:S(2)}) copy-start(bf16[8,4096]{1,0:T(8,128)(2,1)} %param.12) | copy-start | bytes 196612
  18.2 15.5 %copy-start.5 = (s32[1,8]{1,0:T(1,128)S(1)}, s32[1,8]{1,0:T(1,128)}, u32[]{:S(2)}) copy-start(s32[1,8]{1,0:T(1,128)} %param.15) | copy-start | bytes 100
  33.9 10.5 %all-to-all-start.1 = ((bf16[8,2,3584]{2,1,0:T(2,128)(2,1)}), bf16[8,2,3584]{2,1,0:T(2,128)(2,1)S(1)}, u32[]{:S(2)}, u32[]{:S(2)}) async-start(bf16[8,2,3584]{2,1,0:T(2,128)(2,1)} %shard_map.122), calls=%async_computation.1 | async-start | bytes 229376 | tf_op jit(solution)/shard_map/all_to_all | solution.py:117
  37.3 1.4 %copy-start.3 = (bf16[64,2048]{1,0:T(8,128)(2,1)S(1)}, bf16[64,2048]{1,0:T(8,128)(2,1)}, u32[]{:S(2)}) copy-start(bf16[64,2048]{1,0:T(8,128)(2,1)} %param.14) | copy-start | bytes 786436
  39.6 1.9 %copy-start.1 = (f32[512,2048]{1,0:T(8,128)}, f32[512,2048]{1,0:T(8,128)S(1)}, u32[]{:S(2)}) copy-start(f32[512,2048]{1,0:T(8,128)S(1)} %get-tuple-element.11) | copy-start | bytes 12582916
  44.5 4.6 %collective-permute-start = (f32[2,3584]{1,0:T(2,128)S(1)}, f32[2,3584]{1,0:T(2,128)S(1)}, u32[]{:S(2)}, u32[]{:S(2)}) collective-permute-start(f32[2,3584]{1,0:T(2,128)S(1)} %convert_reduce_fusion), channel_id=1, source_target_pairs={{0,1},{1,0},{2,3},{3,2},{4,5},{5,4},{6,7},{7,6},{8,9},{9,8},{10,11... | collective-permute-start | bytes 86024 | tf_op jit(solution)/shard_map/ppermute | solution.py:119

commit v2 on v1

v2 whole, which is shorter than its diff:
```python
import jax
import jax.numpy as jnp
from jax import lax
from jax.experimental import pallas as pl
from jax.experimental.pallas import tpu as pltpu
from jax.sharding import PartitionSpec as P

EXPERTS = 16
LANES = 128
MIB = 1 << 20

score_scale = 192.0 ** (-0.5)
LOG2E = 1.4426950408889634


def on_chip(count):
    return [pl.BlockSpec(memory_space=pltpu.VMEM)] * count


def in_hbm(array):
    return pltpu.with_memory_space_constraint(array, pltpu.HBM)


def attend_rows(first, count, lengths_ref, q_ref, q_rope_ref, latent_ref, rope_ref, scores, shares):
    rows, total = scores.shape
    heads_here = rows // count
    block = min(256, total)
    position = lax.broadcasted_iota(jnp.int32, (1, total), 1)
    bias, begin = [], jnp.int32(0)
    for r in range(first + count):
        end = begin + lengths_ref[0, r]
        if r >= first:
            bias.append(jnp.where((position >= begin) & (position < end), 0.0, -jnp.inf))
        begin = end
    highest = [jnp.full((heads_here, LANES), -jnp.inf, jnp.float32)] * count
    mine = slice(first * heads_here, first * heads_here + rows)
    for k in range(0, total, block):
        part = lax.dot_general(
            q_ref[mine, :], latent_ref[k : k + block, :], (((1,), (1,)), ((), ())), preferred_element_type=jnp.float32
        ) + jnp.dot(q_rope_ref[mine, :], rope_ref[:, k : k + block], preferred_element_type=jnp.float32)
        for r in range(count):
            own = slice(r * heads_here, (r + 1) * heads_here)
            masked = part[own] + bias[r][:, k : k + block]
            scores[own, k : k + block] = masked
            for j in range(0, block, LANES):
                highest[r] = jnp.maximum(highest[r], masked[:, j : j + LANES])
    scale = score_scale * LOG2E
    for r in range(count):
        own = slice(r * heads_here, (r + 1) * heads_here)
        top = jnp.max(highest[r], axis=1, keepdims=True) * scale
        weights = jnp.exp2(scores[own, :] * scale - top)
        share = 1.0 / jnp.sum(weights, axis=1, keepdims=True)
        shares[own, :] = (weights * share).astype(jnp.bfloat16)
    return jnp.dot(shares[...], latent_ref[...], preferred_element_type=jnp.float32).astype(jnp.bfloat16)


def attend(first, count, queries, rope_queries, latent, rope_keys, lengths, *before):
    requests = lengths.shape[1]
    rows, total = queries.shape[0] // requests * count, latent.shape[0]
    earlier = sum(b.shape[0] for b in before)

    def kernel(lengths_ref, q_ref, q_rope_ref, latent_ref, rope_ref, *refs):
        out_ref, scores, shares = refs[-3:]
        for ref in refs[:-3]:
            out_ref[:earlier, :] = ref[...]
        out_ref[earlier:, :] = attend_rows(
            first, count, lengths_ref, q_ref, q_rope_ref, latent_ref, rope_ref, scores, shares
        )

    return pl.pallas_call(
        kernel,
        out_shape=jax.ShapeDtypeStruct((earlier + rows, queries.shape[1]), jnp.bfloat16),
        in_specs=[pl.BlockSpec(memory_space=pltpu.SMEM)] + on_chip(4 + len(before)),
        out_specs=pl.BlockSpec(memory_space=pltpu.VMEM),
        scratch_shapes=[pltpu.VMEM((rows, total), jnp.float32), pltpu.VMEM((rows, total), jnp.bfloat16)],
        compiler_params=pltpu.CompilerParams(vmem_limit_bytes=14 * MIB),
        cost_estimate=pl.CostEstimate(
            flops=2 * rows * total * 1088, bytes_accessed=4 * MIB, transcendentals=rows * total
        ),
    )(lengths, queries, rope_queries, in_hbm(latent), in_hbm(rope_keys), *before)


def cuts(total, most):
    step = next(s for s in (512, 256, 128, 64, 32, 16) if s <= most and total % s == 0)
    return [(k, step) for k in range(0, total, step)]


def pack_kernel(tokens_ref, routes_ref, gates_ref, out_ref, tokens_buf, routes_buf, gates_buf, sems):
    width = tokens_ref.shape[1]
    copies = [
        pltpu.make_async_copy(source, target, sems.at[k])
        for k, (source, target) in enumerate(
            ((tokens_ref, tokens_buf), (routes_ref, routes_buf), (gates_ref, gates_buf))
        )
    ]
    for copy in copies:
        copy.start()
    for copy in copies[1:]:
        copy.wait()
    label = lax.broadcasted_iota(jnp.int32, (tokens_ref.shape[0], LANES), 1)
    table = jnp.zeros(label.shape, jnp.float32)
    for k in range(routes_ref.shape[1]):
        gate = gates_buf[:, k : k + 1].astype(jnp.float32)
        table += jnp.where(routes_buf[:, k : k + 1] == label, gate, 0.0)
    copies[0].wait()
    for j in range(out_ref.shape[0]):
        out_ref[j, :, :width] = tokens_buf[...]
        out_ref[j, :, width:] = table.astype(jnp.bfloat16)


def pack(tokens, routes, gates, copies):
    return pl.pallas_call(
        pack_kernel,
        out_shape=jax.ShapeDtypeStruct((copies, tokens.shape[0], tokens.shape[1] + LANES), tokens.dtype),
        in_specs=[pl.BlockSpec(memory_space=pl.ANY)] * 3,
        out_specs=pl.BlockSpec(memory_space=pltpu.VMEM),
        scratch_shapes=[
            pltpu.VMEM(tokens.shape, tokens.dtype),
            pltpu.VMEM(routes.shape, routes.dtype),
            pltpu.VMEM(gates.shape, gates.dtype),
            pltpu.SemaphoreType.DMA((3,)),
        ],
        compiler_params=pltpu.CompilerParams(vmem_limit_bytes=8 * MIB),
    )(in_hbm(tokens), in_hbm(routes), in_hbm(gates))


def experts(own_expert, share, shares, rows, w_gate, w_up, w_down):
    width = w_down.shape[1]
    ff = w_down.shape[0] // shares
    thin, wide = cuts(width, 512), cuts(ff, 256)

    def kernel(expert_ref, share_ref, rows_ref, gate_ref, up_ref, down_ref, out_ref, gate_buf, up_buf, down_buf, sems):
        begin = pl.multiple_of(share_ref[0] * ff, ff) if shares > 1 else 0
        copies = [[], [], []]
        for n, (source, target) in enumerate(((gate_ref, gate_buf), (up_ref, up_buf), (down_ref, down_buf))):
            for k, step in wide if n == 2 else thin:
                place = (pl.ds(begin + k, step), slice(None)) if n == 2 else (pl.ds(k, step), pl.ds(begin, ff))
                copy = pltpu.make_async_copy(
                    source.at[place], target.at[pl.ds(k, step)], sems.at[sum(map(len, copies))]
                )
                copy.start()
                copies[n].append(copy)
        count = rows_ref.shape[0] * rows_ref.shape[1]
        packed = rows_ref[...].reshape(count, rows_ref.shape[2])
        table = packed[:, width:].astype(jnp.float32)
        label = lax.broadcasted_iota(jnp.int32, table.shape, 1)
        weight = jnp.sum(jnp.where(label == expert_ref[0], table, 0.0), axis=1, keepdims=True)

        def against(left, parts, waits, buf):
            total = 0.0
            for (k, step), copy in zip(parts, waits):
                copy.wait()
                total += jnp.dot(left[:, k : k + step], buf[k : k + step, :], preferred_element_type=jnp.float32)
            return total

        gate_pre = against(packed, thin, copies[0], gate_buf)
        up_pre = against(packed, thin, copies[1], up_buf)
        hidden = (gate_pre / (1.0 + jnp.exp(-gate_pre)) * up_pre).astype(jnp.bfloat16)
        total = against(hidden, wide, copies[2], down_buf)
        out_ref[...] = (total * weight).astype(jnp.bfloat16).reshape(out_ref.shape)

    return pl.pallas_call(
        kernel,
        out_shape=jax.ShapeDtypeStruct(rows.shape[:2] + (width,), jnp.bfloat16),
        in_specs=[pl.BlockSpec(memory_space=pltpu.SMEM)] * 2
        + on_chip(1)
        + [pl.BlockSpec(memory_space=pl.ANY)] * 3,
        out_specs=pl.BlockSpec(memory_space=pltpu.VMEM),
        scratch_shapes=[
            pltpu.VMEM((width, ff), w_gate.dtype),
            pltpu.VMEM((width, ff), w_up.dtype),
            pltpu.VMEM((ff, width), w_down.dtype),
            pltpu.SemaphoreType.DMA((2 * len(thin) + len(wide),)),
        ],
        compiler_params=pltpu.CompilerParams(vmem_limit_bytes=6 * width * ff + 10 * MIB),
    )(own_expert[None], share[None], rows, in_hbm(w_gate), in_hbm(w_up), in_hbm(w_down))


def local(q_latent, q_rope, cache_latent, cache_rope, lengths, tokens_b, routes, gates, w_gate, w_up, w_down):
    latent_width = cache_latent.shape[1]
    requests = lengths.shape[1]
    pool_count = lax.axis_size("pool")
    head_count = lax.axis_size("heads")
    slices = pool_count * head_count // EXPERTS
    own_pool = lax.axis_index("pool")
    own_expert = (own_pool * head_count + lax.axis_index("heads")) // slices

    group_count = lax.axis_size("groups")
    apart = w_down.shape[0] % (group_count * 256) == 0
    shares, axes = (group_count, ("groups", "pool")) if apart else (1, ("pool",))
    packed = pack(tokens_b, routes, gates, pool_count * shares)
    rows = lax.all_to_all(packed, axes, split_axis=0, concat_axis=0, tiled=True)
    queries = q_latent.reshape(-1, latent_width)
    rope_queries = q_rope.reshape(queries.shape[0], cache_rope.shape[0])
    half = requests // 2
    early = attend(0, half, queries, rope_queries, cache_latent, cache_rope, lengths)
    rows, early, queries, rope_queries = lax.optimization_barrier((rows, early, queries, rope_queries))
    share = lax.axis_index("groups").astype(jnp.int32)
    terms = experts(own_expert, share, shares, rows, w_gate, w_up, w_down)
    terms, queries, rope_queries = lax.optimization_barrier((terms, queries, rope_queries))
    returned = lax.all_to_all(terms, axes, split_axis=0, concat_axis=0, tiled=True)
    attended = attend(half, requests - half, queries, rope_queries, cache_latent, cache_rope, lengths, early)
    attended = attended.reshape(requests, -1)
    returned, attended = lax.optimization_barrier((returned, attended))
    local_sum = jnp.sum(returned.astype(jnp.float32), axis=0)
    other = lax.ppermute(local_sum, "heads", [(0, 1), (1, 0)])
    moe_out = (local_sum + other).astype(jnp.bfloat16)
    return (attended, moe_out)


def solution(mesh):
    rows = P(("groups", "pool"), None)
    split = P(("groups", "pool"), "heads")
    placed = (split, split, rows, P(None, ("groups", "pool")), rows, rows, rows, rows)
    weights = (P(None, ("pool", "heads")),) * 2 + (P(("pool", "heads"), None),)
    return jax.shard_map(
        local, mesh=mesh, in_specs=placed + weights, out_specs=(split, rows), check_vma=False
    )
```

time: 50.4 us -> 43.7 us (0.87)
  matrix products: 5.72 us -> 0 us
  other arithmetic: 3.99 us -> 0.81 us
  Pallas kernels: 15.1 us -> 17.4 us
  starting transfers between devices: 10.7 us -> 12.6 us
  waiting for transfers between devices: 9.47 us -> 7.64 us
    dot_general x3 -> x0, matrix products: 5.72 us -> none  [the longest x1 3.51 us: attend(): jnp.dot(shares, latent, preferred_element_type=jnp.float32)]
    all_to_all x2, waiting for transfers between devices: 9.46 us -> 6.46 us  [the longest x1 3.68 us: local(): lax.all_to_all(terms, axes, split_axis=0, concat_axis=0, tiled=True)]
    pallas_call x1 -> x4, Pallas kernels: 15.1 us -> 17.4 us  [the longest x1 8.62 us: experts(): pl.pallas_call(kernel, out_shape=jax.ShapeDtypeStruct(rows.shape[:2] + (w...]
    all_to_all x2, starting transfers between devices: 10.6 us -> 12.5 us  [the longest x1 8.32 us: local(): rows = lax.all_to_all(packed, axes, split_axis=0, concat_axis=0, tiled=True)]
    reduce_sum x2 -> x0, other arithmetic: 1.47 us -> none  [the longest x1 0.76 us: expert_weights(): return jnp.sum(gates.astype(jnp.float32)[:, :, None] * chosen, axis=1)]
    unnamed x12 -> x4, local copies, waits for them, and re-layouts: 1.95 us -> 0.65 us
    ppermute x1, waiting for transfers between devices: 0.01 us -> 1.19 us  [local(): other = lax.ppermute(local_sum, 'heads', [(0, 1), (1, 0)])]
    reshape x1, local copies, waits for them, and re-layouts: 0.24 us -> 1.29 us  [local(): queries = q_latent.reshape(-1, latent_width)]
  transfers between devices with their start and end apart: 3 -> 3, of which waited for: 2 -> 3; matrix products, arithmetic and copies ran while one was open for 15% -> 8% of each run, Pallas kernels for 0% -> 17%
where the time goes in v2:
time: 43.7 us; the launch traced here: 43.2 us
  Pallas kernels  17.4 us (40%)
  starting transfers between devices  12.6 us (29%)
  waiting for transfers between devices  7.64 us (17%)
  local copies, waits for them, and re-layouts  4 us (9%)
  other arithmetic  0.81 us (2%)
  between operations  0.73 us (2%)
    pallas_call x1, Pallas kernels, experts(): pl.pallas_call(kernel, out_shape=jax.ShapeDtypeStruct(rows.shape[:2] + (w...  8.62 us
    all_to_all x1, starting transfers between devices, local(): rows = lax.all_to_all(packed, axes, split_axis=0, concat_axis=0, tiled=True)  8.32 us
    pallas_call x2, Pallas kernels, attend(): pl.pallas_call(kernel, out_shape=jax.ShapeDtypeStruct((earlier + rows, qu...  7.28 us
    all_to_all x1, starting transfers between devices, local(): lax.all_to_all(terms, axes, split_axis=0, concat_axis=0, tiled=True)  4.17 us
    all_to_all x1, waiting for transfers between devices, local(): lax.all_to_all(terms, axes, split_axis=0, concat_axis=0, tiled=True)  3.68 us
    all_to_all x1, waiting for transfers between devices, local(): rows = lax.all_to_all(packed, axes, split_axis=0, concat_axis=0, tiled=True)  2.78 us
    pallas_call x1, Pallas kernels, pack(): pl.pallas_call(pack_kernel, out_shape=jax.ShapeDtypeStruct((copies, token...  1.53 us
    reshape x1, local copies, waits for them, and re-layouts, local(): queries = q_latent.reshape(-1, latent_width)  1.29 us
  transfers between devices with their start and end apart: 3, of which 3 were waited for; matrix products, arithmetic and copies ran while one was open for 8% of the time, Pallas kernels for 17%

profile of v2, /device:TPU:0, one launch (start us, length us, event | category | flops | bytes accessed | tf_op | source)
XLA Modules:
  0.0 43.2 jit_solution(15328769686480008838)
XLA Ops:
  0.6 1.5 %shard_map.122 = bf16[16,2,3712]{2,1,0:T(2,128)(2,1)} custom-call(bf16[2,3584]{1,0:T(2,128)(2,1)} %tokens_ref.1, s32[2,8]{1,0:T(2,128)} %routes_ref.1, bf16[2,8]{1,0:T(2,128)(2,1)} %gates_ref.1), custom_call_target="tpu_custom_call" | custom-call | tf_op jit(solution)/shard_map/pallas_call | solution.py:112
  2.2 8.3 %all-to-all-start = ((bf16[16,2,3712]{2,1,0:T(2,128)(2,1)}), bf16[16,2,3712]{2,1,0:T(2,128)(2,1)S(1)}, u32[]{:S(2)}, u32[]{:S(2)}) async-start(bf16[16,2,3712]{2,1,0:T(2,128)(2,1)} %shard_map.122), calls=%async_computation | async-start | bytes 475136 | tf_op jit(solution)/shard_map/all_to_all | solution.py:192
  10.5 1.0 %reshape.14.q_rope_ref = bf16[512,64]{1,0:T(8,128)(2,1)S(1)} reshape(bf16[8,4096]{1,0:T(8,128)(2,1)} %param.12) | data formatting | bytes 131072 | tf_op jit(solution)/shard_map/reshape | solution.py:194
  11.5 1.3 %reshape.13.q_ref = bf16[512,512]{1,0:T(8,128)(2,1)S(1)} reshape(bf16[8,32768]{1,0:T(8,128)(2,1)} %param.11) | data formatting | bytes 1048576 | tf_op jit(solution)/shard_map/reshape | solution.py:193
  12.8 0.0 copy-start
  12.8 0.6 %copy-done = s32[1,8]{1,0:T(1,128)S(1)} copy-done((s32[1,8]{1,0:T(1,128)S(1)}, s32[1,8]{1,0:T(1,128)}, u32[]{:S(2)}) %copy-start) | copy-done | bytes 56
  13.5 3.6 %shard_map.123.refs_0_ = bf16[256,512]{1,0:T(8,128)(2,1)S(1)} custom-call(s32[1,8]{1,0:T(1,128)S(1)} %copy-done, bf16[512,512]{1,0:T(8,128)(2,1)S(1)} %reshape.13.q_ref, bf16[512,64]{1,0:T(8,128)(2,1)S(1)} %reshape.14.q_rope_ref, bf16[2048,512]{1,0:T(8,128)(2,1)} %latent_ref.3, bf16[64,2048]{1,0:T(8,128)(2,1)} %rope_ref.3), custom_call_target="tpu_custom_call" | custom-call | flops 1140850688 | bytes 4194304 | tf_op jit(solution)/shard_map/pallas_call | solution.py:70
  17.1 2.8 %all-to-all-done.rows_ref = bf16[16,2,3712]{2,1,0:T(2,128)(2,1)S(1)} async-done(((bf16[16,2,3712]{2,1,0:T(2,128)(2,1)}), bf16[16,2,3712]{2,1,0:T(2,128)(2,1)S(1)}, u32[]{:S(2)}, u32[]{:S(2)}) %all-to-all-start) | async-done | bytes 237600 | tf_op jit(solution)/shard_map/all_to_all | solution.py:192
  19.9 0.0 copy-start.1
  19.9 8.6 %shard_map.124 = bf16[16,2,3584]{2,1,0:T(2,128)(2,1)} custom-call(s32[1]{0:T(128)} %bitcast.expert_ref, s32[1]{0:T(128)} %bitcast.1.share_ref, bf16[16,2,3712]{2,1,0:T(2,128)(2,1)S(1)} %all-to-all-done.rows_ref, bf16[3584,2048]{1,0:T(8,128)(2,1)} %gate_ref.1, bf16[3584,2048]{1,0:T(8,128)(2,1)} %up_ref.1, bf16[2048,3584]{1,0:T(8,128)(2,1)} %down_ref.1), custom_call_target="tpu_custom_call" | custom-call | tf_op jit(solution)/shard_map/pallas_call | solution.py:162
  28.5 4.2 %all-to-all-start.1 = ((bf16[16,2,3584]{2,1,0:T(2,128)(2,1)}), bf16[16,2,3584]{2,1,0:T(2,128)(2,1)S(1)}, u32[]{:S(2)}, u32[]{:S(2)}) async-start(bf16[16,2,3584]{2,1,0:T(2,128)(2,1)} %shard_map.124), calls=%async_computation.1 | async-start | bytes 458752 | tf_op jit(solution)/shard_map/all_to_all | solution.py:201
  32.7 0.0 copy-done.1
  32.7 3.7 %shard_map.125 = bf16[512,512]{1,0:T(8,128)(2,1)S(1)} custom-call(s32[1,8]{1,0:T(1,128)S(1)} %copy-done.1, bf16[512,512]{1,0:T(8,128)(2,1)S(1)} %reshape.13.q_ref, bf16[512,64]{1,0:T(8,128)(2,1)S(1)} %reshape.14.q_rope_ref, bf16[2048,512]{1,0:T(8,128)(2,1)} %latent_ref.3, bf16[64,2048]{1,0:T(8,128)(2,1)} %rope_ref.3, bf16[256,512]{1,0:T(8,128)(2,1)S(1)} %shard_map.123.refs_0_), custom_call_target="tpu_custom_call" | custom-call | flops 1140850688 | bytes 4194304 | tf_op jit(solution)/shard_map/pallas_call | solution.py:70
  36.4 1.0 %reshape.15 = bf16[8,32768]{1,0:T(8,128)(2,1)} reshape(bf16[512,512]{1,0:T(8,128)(2,1)S(1)} %shard_map.125) | data formatting | bytes 1048576 | tf_op jit(solution)/shard_map/reshape | solution.py:203
  37.4 3.7 %all-to-all-done.1 = bf16[16,2,3584]{2,1,0:T(2,128)(2,1)S(1)} async-done(((bf16[16,2,3584]{2,1,0:T(2,128)(2,1)}), bf16[16,2,3584]{2,1,0:T(2,128)(2,1)S(1)}, u32[]{:S(2)}, u32[]{:S(2)}) %all-to-all-start.1) | async-done | bytes 229408 | tf_op jit(solution)/shard_map/all_to_all | solution.py:201
  41.1 0.2 convert_reduce_fusion
  41.3 0.1 collective-permute-start
  41.4 1.2 %collective-permute-done = f32[2,3584]{1,0:T(2,128)S(1)} collective-permute-done((f32[2,3584]{1,0:T(2,128)S(1)}, f32[2,3584]{1,0:T(2,128)S(1)}, u32[]{:S(2)}, u32[]{:S(2)}) %collective-permute-start) | collective-permute-done | bytes 28704 | tf_op jit(solution)/shard_map/ppermute | solution.py:206
  42.6 0.6 %add_convert_fusion = bf16[2,3584]{1,0:T(2,128)(2,1)} fusion(f32[2,3584]{1,0:T(2,128)S(1)} %convert_reduce_fusion, f32[2,3584]{1,0:T(2,128)S(1)} %collective-permute-done), kind=kLoop, calls=%fused_computation.1 | loop fusion | flops 14336 | bytes 71680 | tf_op jit(solution)/shard_map/convert_element_type | solution.py:207
Async XLA Ops:
  2.2 17.7 %all-to-all-start = ((bf16[16,2,3712]{2,1,0:T(2,128)(2,1)}), bf16[16,2,3712]{2,1,0:T(2,128)(2,1)S(1)}, u32[]{:S(2)}, u32[]{:S(2)}) async-start(bf16[16,2,3712]{2,1,0:T(2,128)(2,1)} %shard_map.122), calls=%async_computation | async-start | bytes 475136 | tf_op jit(solution)/shard_map/all_to_all | solution.py:192
  12.8 0.7 %copy-start = (s32[1,8]{1,0:T(1,128)S(1)}, s32[1,8]{1,0:T(1,128)}, u32[]{:S(2)}) copy-start(s32[1,8]{1,0:T(1,128)} %lengths_ref.3) | copy-start | bytes 100
  19.9 12.8 %copy-start.1 = (s32[1,8]{1,0:T(1,128)S(1)}, s32[1,8]{1,0:T(1,128)}, u32[]{:S(2)}) copy-start(s32[1,8]{1,0:T(1,128)} %lengths_ref.3) | copy-start | bytes 100
  28.5 12.6 %all-to-all-start.1 = ((bf16[16,2,3584]{2,1,0:T(2,128)(2,1)}), bf16[16,2,3584]{2,1,0:T(2,128)(2,1)S(1)}, u32[]{:S(2)}, u32[]{:S(2)}) async-start(bf16[16,2,3584]{2,1,0:T(2,128)(2,1)} %shard_map.124), calls=%async_computation.1 | async-start | bytes 458752 | tf_op jit(solution)/shard_map/all_to_all | solution.py:201
  41.3 1.3 %collective-permute-start = (f32[2,3584]{1,0:T(2,128)S(1)}, f32[2,3584]{1,0:T(2,128)S(1)}, u32[]{:S(2)}, u32[]{:S(2)}) collective-permute-start(f32[2,3584]{1,0:T(2,128)S(1)} %convert_reduce_fusion), channel_id=1, source_target_pairs={{0,1},{1,0},{2,3},{3,2},{4,5},{5,4},{6,7},{7,6},{8,9},{9,8},{10,11... | collective-permute-start | bytes 86024 | tf_op jit(solution)/shard_map/ppermute | solution.py:206

commit v3 on v2

v3 whole, which is shorter than its diff:
```python
import jax
import jax.numpy as jnp
from jax import lax
from jax.experimental import pallas as pl
from jax.experimental.pallas import tpu as pltpu
from jax.sharding import PartitionSpec as P

EXPERTS = 16
LANES = 128
MIB = 1 << 20
EARLY = 3 * MIB

score_scale = 192.0 ** (-0.5)
LOG2E = 1.4426950408889634


def on_chip(count):
    return [pl.BlockSpec(memory_space=pltpu.VMEM)] * count


def in_hbm(array):
    return pltpu.with_memory_space_constraint(array, pltpu.HBM)


def attend(part, parts, q_latent, q_rope, latent, rope_keys, lengths, done, weight, share, early):
    requests, total, latent_width = lengths.shape[1], latent.shape[0], latent.shape[1]
    rope_width = rope_keys.shape[0]
    heads_here = q_latent.shape[1] // latent_width // parts
    rows = heads_here * requests
    block = min(512, total)
    wide, thin = heads_here * latent_width, heads_here * rope_width
    ff = early[0].shape[1] if early else 0
    chunks = [(k, block) for k in range(0, total, block)]

    def kernel(share_ref, lengths_ref, q_ref, q_rope_ref, latent_ref, rope_ref, *refs):
        rest = len(done) + (1 if early else 0)
        out_ref, piece_refs = refs[rest], refs[rest + 1 : rest + 1 + len(early)]
        (lengths_buf, q_buf, q_rope_buf, latent_buf, rope_buf, tall, tall_rope, scores, out_buf, sems) = refs[
            rest + 1 + len(early) :
        ]
        pairs = [
            (lengths_ref, lengths_buf),
            (q_ref.at[:, pl.ds(part * wide, wide)], q_buf),
            (q_rope_ref.at[:, pl.ds(part * thin, thin)], q_rope_buf),
            (rope_ref, rope_buf),
        ] + [(latent_ref.at[pl.ds(k, n)], latent_buf.at[pl.ds(k, n)]) for k, n in chunks]
        if early:
            begin = pl.multiple_of(share_ref[0] * ff, LANES)
            for k, piece_ref in enumerate(piece_refs):
                n = piece_ref.shape[0]
                pairs.append((refs[len(done)].at[pl.ds(k * n, n), pl.ds(begin, ff)], piece_ref))
        copies = [pltpu.make_async_copy(source, target, sems.at[k]) for k, (source, target) in enumerate(pairs)]
        for copy in copies:
            copy.start()
        for copy in copies[:4]:
            copy.wait()
        for h in range(heads_here):
            own = slice(h * requests, (h + 1) * requests)
            tall[own, :] = q_buf[:, h * latent_width : (h + 1) * latent_width].astype(jnp.float32)
            tall_rope[own, :] = q_rope_buf[:, h * rope_width : (h + 1) * rope_width].astype(jnp.float32)
        queries, rope_queries = tall[...].astype(jnp.bfloat16), tall_rope[...].astype(jnp.bfloat16)
        request = lax.broadcasted_iota(jnp.int32, (requests, 1), 0)
        begin, end, start = jnp.zeros_like(request), jnp.zeros_like(request), jnp.int32(0)
        for r in range(requests):
            begin = jnp.where(request == r, start, begin)
            start = start + lengths_buf[0, r]
            end = jnp.where(request == r, start, end)
        position = lax.broadcasted_iota(jnp.int32, (requests, total), 1)
        bias = jnp.where((position >= begin) & (position < end), 0.0, -jnp.inf)
        highest = jnp.full((heads_here, requests, LANES), -jnp.inf, jnp.float32)
        for (k, n), copy in zip(chunks, copies[4:]):
            copy.wait()
            part_scores = lax.dot_general(
                queries, latent_buf[k : k + n, :], (((1,), (1,)), ((), ())), preferred_element_type=jnp.float32
            ) + jnp.dot(rope_queries, rope_buf[:, k : k + n], preferred_element_type=jnp.float32)
            masked = part_scores.reshape(heads_here, requests, n) + bias[None, :, k : k + n]
            scores[:, k : k + n] = masked.reshape(rows, n)
            for j in range(0, n, LANES):
                highest = jnp.maximum(highest, masked[:, :, j : j + LANES])
        scale = score_scale * LOG2E
        top = jnp.max(highest, axis=2, keepdims=True).reshape(rows, 1) * scale
        step = 64
        for k in range(0, rows, step):
            own = slice(k, k + step)
            weights = jnp.exp2(scores[own, :] * scale - top[own])
            shares = (weights * (1.0 / jnp.sum(weights, axis=1, keepdims=True))).astype(jnp.bfloat16)
            result = jnp.dot(shares, latent_buf[...], preferred_element_type=jnp.float32)
            for j in range(0, step, requests):
                h = (k + j) // requests
                out_buf[:, h * latent_width : (h + 1) * latent_width] = result[j : j + requests].astype(jnp.bfloat16)
        last = pltpu.make_async_copy(out_buf, out_ref.at[:, pl.ds(part * wide, wide)], sems.at[len(pairs)])
        last.start()
        for copy in copies[4 + len(chunks) :]:
            copy.wait()
        last.wait()

    extra = [in_hbm(weight)] if early else []
    return pl.pallas_call(
        kernel,
        out_shape=[pltpu.HBM(q_latent.shape, jnp.bfloat16)] + [pltpu.VMEM(e.shape, e.dtype) for e in early],
        in_specs=[pl.BlockSpec(memory_space=pltpu.SMEM)]
        + [pl.BlockSpec(memory_space=pl.ANY)] * (5 + len(done) + len(extra)),
        out_specs=[pl.BlockSpec(memory_space=pl.ANY)] + on_chip(len(early)),
        input_output_aliases={6: 0} if done else {},
        scratch_shapes=[
            pltpu.SMEM(lengths.shape, lengths.dtype),
            pltpu.VMEM((requests, wide), jnp.bfloat16),
            pltpu.VMEM((requests, thin), jnp.bfloat16),
            pltpu.VMEM(latent.shape, latent.dtype),
            pltpu.VMEM(rope_keys.shape, rope_keys.dtype),
            pltpu.VMEM((rows, latent_width), jnp.float32),
            pltpu.VMEM((rows, rope_width), jnp.float32),
            pltpu.VMEM((rows, total), jnp.float32),
            pltpu.VMEM((requests, wide), jnp.bfloat16),
            pltpu.SemaphoreType.DMA((5 + len(chunks) + len(early),)),
        ],
        compiler_params=pltpu.CompilerParams(vmem_limit_bytes=16 * MIB),
        cost_estimate=pl.CostEstimate(
            flops=2 * rows * total * (2 * latent_width + rope_width),
            bytes_accessed=4 * MIB,
            transcendentals=rows * total,
        ),
    )(share[None], *[in_hbm(x) for x in (lengths, q_latent, q_rope, latent, rope_keys)], *done, *extra)


def cuts(total, most):
    step = next(s for s in (512, 256, 128, 64, 32, 16) if s <= most and total % s == 0)
    return [(k, step) for k in range(0, total, step)]


def pack_kernel(tokens_ref, routes_ref, gates_ref, out_ref, tokens_buf, routes_buf, gates_buf, sems):
    width = tokens_ref.shape[1]
    copies = [
        pltpu.make_async_copy(source, target, sems.at[k])
        for k, (source, target) in enumerate(
            ((tokens_ref, tokens_buf), (routes_ref, routes_buf), (gates_ref, gates_buf))
        )
    ]
    for copy in copies:
        copy.start()
    for copy in copies[1:]:
        copy.wait()
    label = lax.broadcasted_iota(jnp.int32, (tokens_ref.shape[0], LANES), 1)
    table = jnp.zeros(label.shape, jnp.float32)
    for k in range(routes_ref.shape[1]):
        gate = gates_buf[:, k : k + 1].astype(jnp.float32)
        table += jnp.where(routes_buf[:, k : k + 1] == label, gate, 0.0)
    copies[0].wait()
    for j in range(out_ref.shape[0]):
        out_ref[j, :, :width] = tokens_buf[...]
        out_ref[j, :, width:] = table.astype(jnp.bfloat16)


def pack(tokens, routes, gates, copies):
    return pl.pallas_call(
        pack_kernel,
        out_shape=jax.ShapeDtypeStruct((copies, tokens.shape[0], tokens.shape[1] + LANES), tokens.dtype),
        in_specs=[pl.BlockSpec(memory_space=pl.ANY)] * 3,
        out_specs=pl.BlockSpec(memory_space=pltpu.VMEM),
        scratch_shapes=[
            pltpu.VMEM(tokens.shape, tokens.dtype),
            pltpu.VMEM(routes.shape, routes.dtype),
            pltpu.VMEM(gates.shape, gates.dtype),
            pltpu.SemaphoreType.DMA((3,)),
        ],
        compiler_params=pltpu.CompilerParams(vmem_limit_bytes=8 * MIB),
    )(in_hbm(tokens), in_hbm(routes), in_hbm(gates))


def experts(own_expert, share, shares, rows, w_gate, w_up, w_down, early):
    width = w_down.shape[1]
    ff = w_down.shape[0] // shares
    thin, wide = cuts(width, 512), cuts(ff, 256)

    def kernel(expert_ref, share_ref, rows_ref, gate_ref, up_ref, down_ref, *refs):
        early_refs, (out_ref, gate_buf, up_buf, down_buf, out_buf, sems) = refs[: len(early)], refs[len(early) :]
        begin = pl.multiple_of(share_ref[0] * ff, ff) if shares > 1 else 0
        copies = [[], [], []]
        for n, (source, target) in enumerate(((gate_ref, gate_buf), (up_ref, up_buf), (down_ref, down_buf))):
            for k, step in wide if n == 2 else thin[0 if n else len(early) :]:
                place = (pl.ds(begin + k, step), slice(None)) if n == 2 else (pl.ds(k, step), pl.ds(begin, ff))
                copy = pltpu.make_async_copy(
                    source.at[place], target.at[pl.ds(k, step)], sems.at[sum(map(len, copies))]
                )
                copy.start()
                copies[n].append(copy)
        count = rows_ref.shape[0] * rows_ref.shape[1]
        packed = rows_ref[...].reshape(count, rows_ref.shape[2])
        table = packed[:, width:].astype(jnp.float32)
        label = lax.broadcasted_iota(jnp.int32, table.shape, 1)
        weight = jnp.sum(jnp.where(label == expert_ref[0], table, 0.0), axis=1, keepdims=True)

        def against(left, parts, waits, buf):
            total = 0.0
            for (k, step), copy in zip(parts, waits):
                copy.wait()
                total += jnp.dot(left[:, k : k + step], buf[k : k + step, :], preferred_element_type=jnp.float32)
            return total

        gate_pre = 0.0
        for (k, step), ref in zip(thin, early_refs):
            gate_pre += jnp.dot(packed[:, k : k + step], ref[...], preferred_element_type=jnp.float32)
        gate_pre += against(packed, thin[len(early) :], copies[0], gate_buf)
        up_pre = against(packed, thin, copies[1], up_buf)
        hidden = (gate_pre / (1.0 + jnp.exp(-gate_pre)) * up_pre).astype(jnp.bfloat16)
        total = against(hidden, wide, copies[2], down_buf)
        out_buf[...] = (total * weight).astype(jnp.bfloat16).reshape(out_buf.shape)
        last = pltpu.make_async_copy(out_buf, out_ref, sems.at[sum(map(len, copies))])
        last.start()
        last.wait()

    return pl.pallas_call(
        kernel,
        out_shape=pltpu.HBM(rows.shape[:2] + (width,), jnp.bfloat16),
        in_specs=[pl.BlockSpec(memory_space=pltpu.SMEM)] * 2
        + on_chip(1)
        + [pl.BlockSpec(memory_space=pl.ANY)] * 3
        + on_chip(len(early)),
        out_specs=pl.BlockSpec(memory_space=pl.ANY),
        scratch_shapes=[
            pltpu.VMEM((width, ff), w_gate.dtype),
            pltpu.VMEM((width, ff), w_up.dtype),
            pltpu.VMEM((ff, width), w_down.dtype),
            pltpu.VMEM(rows.shape[:2] + (width,), jnp.bfloat16),
            pltpu.SemaphoreType.DMA((2 * len(thin) + len(wide) + 1,)),
        ],
        compiler_params=pltpu.CompilerParams(vmem_limit_bytes=6 * width * ff + 10 * MIB),
    )(own_expert[None], share[None], rows, in_hbm(w_gate), in_hbm(w_up), in_hbm(w_down), *early)


def local(q_latent, q_rope, cache_latent, cache_rope, lengths, tokens_b, routes, gates, w_gate, w_up, w_down):
    pool_count = lax.axis_size("pool")
    head_count = lax.axis_size("heads")
    slices = pool_count * head_count // EXPERTS
    own_pool = lax.axis_index("pool")
    own_expert = (own_pool * head_count + lax.axis_index("heads")) // slices

    group_count = lax.axis_size("groups")
    apart = w_down.shape[0] % (group_count * 256) == 0
    shares, axes = (group_count, ("groups", "pool")) if apart else (1, ("pool",))
    packed = pack(tokens_b, routes, gates, pool_count * shares)
    rows = lax.all_to_all(packed, axes, split_axis=0, concat_axis=0, tiled=True)
    share = lax.axis_index("groups").astype(jnp.int32) if apart else jnp.int32(0)
    ff = w_down.shape[0] // shares
    model_width = tokens_b.shape[1]
    step = cuts(model_width, 512)[0][1]
    pieces = min(model_width // step, EARLY // (2 * step * ff))
    pieces = [jax.ShapeDtypeStruct((step, ff), w_gate.dtype)] * pieces
    inputs = (q_latent, q_rope, cache_latent, cache_rope, lengths)
    half, *early = attend(0, 2, *inputs, [], w_gate, share, pieces)
    rows, half, *early = lax.optimization_barrier((rows, half, *early))
    terms = experts(own_expert, share, shares, rows, w_gate, w_up, w_down, early)
    terms, half = lax.optimization_barrier((terms, half))
    returned = lax.all_to_all(terms, axes, split_axis=0, concat_axis=0, tiled=True)
    (attended,) = attend(1, 2, *inputs, [half], w_gate, share, [])
    returned, attended = lax.optimization_barrier((returned, attended))
    local_sum = jnp.sum(returned.astype(jnp.float32), axis=0)
    other = lax.ppermute(local_sum, "heads", [(0, 1), (1, 0)])
    moe_out = (local_sum + other).astype(jnp.bfloat16)
    return (attended, moe_out)


def solution(mesh):
    rows = P(("groups", "pool"), None)
    split = P(("groups", "pool"), "heads")
    placed = (split, split, rows, P(None, ("groups", "pool")), rows, rows, rows, rows)
    weights = (P(None, ("pool", "heads")),) * 2 + (P(("pool", "heads"), None),)
    return jax.shard_map(
        local, mesh=mesh, in_specs=placed + weights, out_specs=(split, rows), check_vma=False
    )
```

time: 43.7 us -> 42.4 us (0.970)
  local copies, waits for them, and re-layouts: 4 us -> 0 us
  Pallas kernels: 17.4 us -> 20 us
  waiting for transfers between devices: 7.64 us -> 8.47 us
  starting transfers between devices: 12.6 us -> 11.9 us
    reshape x3 -> x0, local copies, waits for them, and re-layouts: 3.35 us -> none  [the longest x1 1.29 us: local(): queries = q_latent.reshape(-1, latent_width)]
    pallas_call x3, Pallas kernels: 15.9 us -> 18.5 us  [the longest x2 10.4 us: attend(): pl.pallas_call(kernel, out_shape=[pltpu.HBM(q_latent.shape, jnp.bfloat16)...]
    all_to_all x1, waiting for transfers between devices: 2.78 us -> 4.17 us  [local(): rows = lax.all_to_all(packed, axes, split_axis=0, concat_axis=0, tiled=True)]
    unnamed x4 -> x0, local copies, waits for them, and re-layouts: 0.65 us -> none
    all_to_all x1, starting transfers between devices: 4.17 us -> 3.54 us  [local(): lax.all_to_all(terms, axes, split_axis=0, concat_axis=0, tiled=True)]
    all_to_all x1, waiting for transfers between devices: 3.68 us -> 3.11 us  [local(): lax.all_to_all(terms, axes, split_axis=0, concat_axis=0, tiled=True)]
  transfers between devices with their start and end apart: 3 -> 3, of which waited for: 3 -> 3; matrix products, arithmetic and copies ran while one was open for 8% -> 0% of each run, Pallas kernels for 17% -> 25%
where the time goes in v3:
time: 42.4 us; the launch traced here: 41.9 us
  Pallas kernels  20 us (47%)
  starting transfers between devices  11.9 us (28%)
  waiting for transfers between devices  8.47 us (20%)
  other arithmetic  0.81 us (2%)
  between operations  0.7 us (2%)
    pallas_call x2, Pallas kernels, attend(): pl.pallas_call(kernel, out_shape=[pltpu.HBM(q_latent.shape, jnp.bfloat16)...  10.4 us
    all_to_all x1, starting transfers between devices, local(): rows = lax.all_to_all(packed, axes, split_axis=0, concat_axis=0, tiled=True)  8.32 us
    pallas_call x1, Pallas kernels, experts(): pl.pallas_call(kernel, out_shape=pltpu.HBM(rows.shape[:2] + (width,), jnp...  8.11 us
    all_to_all x1, waiting for transfers between devices, local(): rows = lax.all_to_all(packed, axes, split_axis=0, concat_axis=0, tiled=True)  4.17 us
    all_to_all x1, starting transfers between devices, local(): lax.all_to_all(terms, axes, split_axis=0, concat_axis=0, tiled=True)  3.54 us
    all_to_all x1, waiting for transfers between devices, local(): lax.all_to_all(terms, axes, split_axis=0, concat_axis=0, tiled=True)  3.11 us
    pallas_call x1, Pallas kernels, pack(): pl.pallas_call(pack_kernel, out_shape=jax.ShapeDtypeStruct((copies, token...  1.52 us
    ppermute x1, waiting for transfers between devices, local(): other = lax.ppermute(local_sum, 'heads', [(0, 1), (1, 0)])  1.19 us
  transfers between devices with their start and end apart: 3, of which 3 were waited for; matrix products, arithmetic and copies ran while one was open for 0% of the time, Pallas kernels for 25%

profile of v3, /device:TPU:0, one launch (start us, length us, event | category | flops | bytes accessed | tf_op | source)
XLA Modules:
  0.0 41.9 jit_solution(784620059088845339)
XLA Ops:
  0.6 1.5 %shard_map.122 = bf16[16,2,3712]{2,1,0:T(2,128)(2,1)} custom-call(bf16[2,3584]{1,0:T(2,128)(2,1)} %tokens_ref.1, s32[2,8]{1,0:T(2,128)} %routes_ref.1, bf16[2,8]{1,0:T(2,128)(2,1)} %gates_ref.1), custom_call_target="tpu_custom_call" | custom-call | tf_op jit(solution)/shard_map/pallas_call | solution.py:155
  2.2 8.3 %all-to-all-start = ((bf16[16,2,3712]{2,1,0:T(2,128)(2,1)}), bf16[16,2,3712]{2,1,0:T(2,128)(2,1)S(1)}, u32[]{:S(2)}, u32[]{:S(2)}) async-start(bf16[16,2,3712]{2,1,0:T(2,128)(2,1)} %shard_map.122), calls=%async_computation | async-start | bytes 475136 | tf_op jit(solution)/shard_map/all_to_all | solution.py:242
  10.5 5.2 %shard_map.123 = (bf16[8,32768]{1,0:T(8,128)(2,1)}, bf16[512,1024]{1,0:T(8,128)(2,1)S(1)}, bf16[512,1024]{1,0:T(8,128)(2,1)S(1)}, bf16[512,1024]{1,0:T(8,128)(2,1)S(1)}) custom-call(s32[1]{0:T(128)} %bitcast.1.share_ref, s32[1,8]{1,0:T(1,128)} %lengths_ref.3, bf16[8,32768]{1,0:T(8,128)(2,1)} %q_ref.3, bf16[8,4096]{1,0:T(8,128)(2,1)} %q_rope_ref.3, ...), custom_call_target="tpu_custom_call" | custom-call | flops 1140850688 | bytes 4194304 | tf_op jit(solution)/shard_map/pallas_call | solution.py:98
  15.7 4.2 %all-to-all-done.rows_ref = bf16[16,2,3712]{2,1,0:T(2,128)(2,1)S(1)} async-done(((bf16[16,2,3712]{2,1,0:T(2,128)(2,1)}), bf16[16,2,3712]{2,1,0:T(2,128)(2,1)S(1)}, u32[]{:S(2)}, u32[]{:S(2)}) %all-to-all-start) | async-done | bytes 237600 | tf_op jit(solution)/shard_map/all_to_all | solution.py:242
  19.9 8.1 %shard_map.124 = bf16[16,2,3584]{2,1,0:T(2,128)(2,1)} custom-call(s32[1]{0:T(128)} %bitcast.expert_ref, s32[1]{0:T(128)} %bitcast.1.share_ref, bf16[16,2,3712]{2,1,0:T(2,128)(2,1)S(1)} %all-to-all-done.rows_ref, bf16[3584,2048]{1,0:T(8,128)(2,1)} %gate_ref.1, bf16[3584,2048]{1,0:T(8,128)(2,1)} %up_ref.1, bf16[2048,3584]{1,0:T(8,128)(2,1)} %down_ref.1, ...), custom_call_target="tpu_custom_call" | custom-call | tf_op jit(solution)/shard_map/pallas_call | solution.py:212
  28.0 3.5 %all-to-all-start.1 = ((bf16[16,2,3584]{2,1,0:T(2,128)(2,1)}), bf16[16,2,3584]{2,1,0:T(2,128)(2,1)S(1)}, u32[]{:S(2)}, u32[]{:S(2)}) async-start(bf16[16,2,3584]{2,1,0:T(2,128)(2,1)} %shard_map.124), calls=%async_computation.1 | async-start | bytes 458752 | tf_op jit(solution)/shard_map/all_to_all | solution.py:254
  31.6 5.2 %shard_map.125 = bf16[8,32768]{1,0:T(8,128)(2,1)} custom-call(s32[1]{0:T(128)} %bitcast.1.share_ref, s32[1,8]{1,0:T(1,128)} %lengths_ref.3, bf16[8,32768]{1,0:T(8,128)(2,1)} %q_ref.3, bf16[8,4096]{1,0:T(8,128)(2,1)} %q_rope_ref.3, bf16[2048,512]{1,0:T(8,128)(2,1)} %latent_ref.3, bf16[64,2048]{1,0:T(8,128)(2,1)} %rope_ref.3, ...), custom_call_target="tpu_custom_call", output_to_operand_aliasing={{}: (6, {})} | custom-call | flops 1140850688 | bytes 4194304 | tf_op jit(solution)/shard_map/pallas_call | solution.py:98
  36.8 3.1 %all-to-all-done.1 = bf16[16,2,3584]{2,1,0:T(2,128)(2,1)S(1)} async-done(((bf16[16,2,3584]{2,1,0:T(2,128)(2,1)}), bf16[16,2,3584]{2,1,0:T(2,128)(2,1)S(1)}, u32[]{:S(2)}, u32[]{:S(2)}) %all-to-all-start.1) | async-done | bytes 229408 | tf_op jit(solution)/shard_map/all_to_all | solution.py:254
  39.9 0.2 convert_reduce_fusion
  40.1 0.1 collective-permute-start
  40.1 1.2 %collective-permute-done = f32[2,3584]{1,0:T(2,128)S(1)} collective-permute-done((f32[2,3584]{1,0:T(2,128)S(1)}, f32[2,3584]{1,0:T(2,128)S(1)}, u32[]{:S(2)}, u32[]{:S(2)}) %collective-permute-start) | collective-permute-done | bytes 28704 | tf_op jit(solution)/shard_map/ppermute | solution.py:258
  41.3 0.6 %add_convert_fusion = bf16[2,3584]{1,0:T(2,128)(2,1)} fusion(f32[2,3584]{1,0:T(2,128)S(1)} %convert_reduce_fusion, f32[2,3584]{1,0:T(2,128)S(1)} %collective-permute-done), kind=kLoop, calls=%fused_computation.1 | loop fusion | flops 14336 | bytes 71680 | tf_op jit(solution)/shard_map/convert_element_type | solution.py:259
Async XLA Ops:
  2.2 17.7 %all-to-all-start = ((bf16[16,2,3712]{2,1,0:T(2,128)(2,1)}), bf16[16,2,3712]{2,1,0:T(2,128)(2,1)S(1)}, u32[]{:S(2)}, u32[]{:S(2)}) async-start(bf16[16,2,3712]{2,1,0:T(2,128)(2,1)} %shard_map.122), calls=%async_computation | async-start | bytes 475136 | tf_op jit(solution)/shard_map/all_to_all | solution.py:242
  28.0 11.9 %all-to-all-start.1 = ((bf16[16,2,3584]{2,1,0:T(2,128)(2,1)}), bf16[16,2,3584]{2,1,0:T(2,128)(2,1)S(1)}, u32[]{:S(2)}, u32[]{:S(2)}) async-start(bf16[16,2,3584]{2,1,0:T(2,128)(2,1)} %shard_map.124), calls=%async_computation.1 | async-start | bytes 458752 | tf_op jit(solution)/shard_map/all_to_all | solution.py:254
  40.1 1.3 %collective-permute-start = (f32[2,3584]{1,0:T(2,128)S(1)}, f32[2,3584]{1,0:T(2,128)S(1)}, u32[]{:S(2)}, u32[]{:S(2)}) collective-permute-start(f32[2,3584]{1,0:T(2,128)S(1)} %convert_reduce_fusion), channel_id=1, source_target_pairs={{0,1},{1,0},{2,3},{3,2},{4,5},{5,4},{6,7},{7,6},{8,9},{9,8},{10,11... | collective-permute-start | bytes 86024 | tf_op jit(solution)/shard_map/ppermute | solution.py:258

commit v4 on v3

--- a/solution.py
+++ b/solution.py
@@ -238,8 +238,14 @@
     group_count = lax.axis_size("groups")
     apart = w_down.shape[0] % (group_count * 256) == 0
     shares, axes = (group_count, ("groups", "pool")) if apart else (1, ("pool",))
-    packed = pack(tokens_b, routes, gates, pool_count * shares)
-    rows = lax.all_to_all(packed, axes, split_axis=0, concat_axis=0, tiled=True)
+    peers = pool_count * shares
+    middle = peers * 3 // 4
+    order = [middle] + [i for i in reversed(range(peers)) if i != middle]
+
+    def swap(blocks):
+        return lax.all_to_all(blocks, axes, split_axis=0, concat_axis=0, tiled=True, axis_index_groups=[order])
+
+    rows = swap(pack(tokens_b, routes, gates, peers))
     share = lax.axis_index("groups").astype(jnp.int32) if apart else jnp.int32(0)
     ff = w_down.shape[0] // shares
     model_width = tokens_b.shape[1]
@@ -251,7 +257,7 @@
     rows, half, *early = lax.optimization_barrier((rows, half, *early))
     terms = experts(own_expert, share, shares, rows, w_gate, w_up, w_down, early)
     terms, half = lax.optimization_barrier((terms, half))
-    returned = lax.all_to_all(terms, axes, split_axis=0, concat_axis=0, tiled=True)
+    returned = swap(terms)
     (attended,) = attend(1, 2, *inputs, [half], w_gate, share, [])
     returned, attended = lax.optimization_barrier((returned, attended))
     local_sum = jnp.sum(returned.astype(jnp.float32), axis=0)

time: 42.4 us -> 39.2 us (0.925)
  waiting for transfers between devices: 8.47 us -> 2.48 us
  starting transfers between devices: 11.9 us -> 14.8 us
    all_to_all x2, waiting for transfers between devices: 7.28 us -> 1.29 us  [swap(): lax.all_to_all(blocks, axes, split_axis=0, concat_axis=0, tiled=True, axi...]
    all_to_all x2, starting transfers between devices: 11.9 us -> 14.7 us  [swap(): lax.all_to_all(blocks, axes, split_axis=0, concat_axis=0, tiled=True, axi...]
  transfers between devices with their start and end apart: 3 -> 3, of which waited for: 3 -> 3; matrix products, arithmetic and copies ran while one was open for 0% -> 0% of each run, Pallas kernels for 25% -> 27%
where the time goes in v4:
time: 39.2 us; the launch traced here: 38.8 us
  Pallas kernels  20 us (51%)
  starting transfers between devices  14.8 us (38%)
  waiting for transfers between devices  2.48 us (6%)
  other arithmetic  0.81 us (2%)
  between operations  0.67 us (2%)
    all_to_all x2, starting transfers between devices, swap(): lax.all_to_all(blocks, axes, split_axis=0, concat_axis=0, tiled=True, axi...  14.7 us
    pallas_call x2, Pallas kernels, attend(): pl.pallas_call(kernel, out_shape=[pltpu.HBM(q_latent.shape, jnp.bfloat16)...  10.4 us
    pallas_call x1, Pallas kernels, experts(): pl.pallas_call(kernel, out_shape=pltpu.HBM(rows.shape[:2] + (width,), jnp...  8.11 us
    pallas_call x1, Pallas kernels, pack(): pl.pallas_call(pack_kernel, out_shape=jax.ShapeDtypeStruct((copies, token...  1.52 us
    all_to_all x2, waiting for transfers between devices, swap(): lax.all_to_all(blocks, axes, split_axis=0, concat_axis=0, tiled=True, axi...  1.29 us
    ppermute x1, waiting for transfers between devices, local(): other = lax.ppermute(local_sum, 'heads', [(0, 1), (1, 0)])  1.19 us
  transfers between devices with their start and end apart: 3, of which 3 were waited for; matrix products, arithmetic and copies ran while one was open for 0% of the time, Pallas kernels for 27%

profile of v4, /device:TPU:0, one launch (start us, length us, event | category | flops | bytes accessed | tf_op | source)
XLA Modules:
  0.0 38.8 jit_solution(10859081024961877262)
XLA Ops:
  0.6 1.5 %shard_map.122 = bf16[16,2,3712]{2,1,0:T(2,128)(2,1)} custom-call(bf16[2,3584]{1,0:T(2,128)(2,1)} %tokens_ref.1, s32[2,8]{1,0:T(2,128)} %routes_ref.1, bf16[2,8]{1,0:T(2,128)(2,1)} %gates_ref.1), custom_call_target="tpu_custom_call" | custom-call | tf_op jit(solution)/shard_map/pallas_call | solution.py:155
  2.2 8.8 %all-to-all-start = ((bf16[16,2,3712]{2,1,0:T(2,128)(2,1)}), bf16[16,2,3712]{2,1,0:T(2,128)(2,1)S(1)}, u32[]{:S(2)}, u32[]{:S(2)}) async-start(bf16[16,2,3712]{2,1,0:T(2,128)(2,1)} %shard_map.122), calls=%async_computation | async-start | bytes 475136 | tf_op jit(solution)/shard_map/all_to_all | solution.py:246
  11.0 5.2 %shard_map.123 = (bf16[8,32768]{1,0:T(8,128)(2,1)}, bf16[512,1024]{1,0:T(8,128)(2,1)S(1)}, bf16[512,1024]{1,0:T(8,128)(2,1)S(1)}, bf16[512,1024]{1,0:T(8,128)(2,1)S(1)}) custom-call(s32[1]{0:T(128)} %bitcast.1.share_ref, s32[1,8]{1,0:T(1,128)} %lengths_ref.3, bf16[8,32768]{1,0:T(8,128)(2,1)} %q_ref.3, bf16[8,4096]{1,0:T(8,128)(2,1)} %q_rope_ref.3, ...), custom_call_target="tpu_custom_call" | custom-call | flops 1140850688 | bytes 4194304 | tf_op jit(solution)/shard_map/pallas_call | solution.py:98
  16.2 1.2 %all-to-all-done.rows_ref = bf16[16,2,3712]{2,1,0:T(2,128)(2,1)S(1)} async-done(((bf16[16,2,3712]{2,1,0:T(2,128)(2,1)}), bf16[16,2,3712]{2,1,0:T(2,128)(2,1)S(1)}, u32[]{:S(2)}, u32[]{:S(2)}) %all-to-all-start) | async-done | bytes 237600 | tf_op jit(solution)/shard_map/all_to_all | solution.py:246
  17.4 8.1 %shard_map.124 = bf16[16,2,3584]{2,1,0:T(2,128)(2,1)} custom-call(s32[1]{0:T(128)} %bitcast.expert_ref, s32[1]{0:T(128)} %bitcast.1.share_ref, bf16[16,2,3712]{2,1,0:T(2,128)(2,1)S(1)} %all-to-all-done.rows_ref, bf16[3584,2048]{1,0:T(8,128)(2,1)} %gate_ref.1, bf16[3584,2048]{1,0:T(8,128)(2,1)} %up_ref.1, bf16[2048,3584]{1,0:T(8,128)(2,1)} %down_ref.1, ...), custom_call_target="tpu_custom_call" | custom-call | tf_op jit(solution)/shard_map/pallas_call | solution.py:212
  25.5 5.9 %all-to-all-start.1 = ((bf16[16,2,3584]{2,1,0:T(2,128)(2,1)}), bf16[16,2,3584]{2,1,0:T(2,128)(2,1)S(1)}, u32[]{:S(2)}, u32[]{:S(2)}) async-start(bf16[16,2,3584]{2,1,0:T(2,128)(2,1)} %shard_map.124), calls=%async_computation.1 | async-start | bytes 458752 | tf_op jit(solution)/shard_map/all_to_all | solution.py:246
  31.4 5.2 %shard_map.125 = bf16[8,32768]{1,0:T(8,128)(2,1)} custom-call(s32[1]{0:T(128)} %bitcast.1.share_ref, s32[1,8]{1,0:T(1,128)} %lengths_ref.3, bf16[8,32768]{1,0:T(8,128)(2,1)} %q_ref.3, bf16[8,4096]{1,0:T(8,128)(2,1)} %q_rope_ref.3, bf16[2048,512]{1,0:T(8,128)(2,1)} %latent_ref.3, bf16[64,2048]{1,0:T(8,128)(2,1)} %rope_ref.3, ...), custom_call_target="tpu_custom_call", output_to_operand_aliasing={{}: (6, {})} | custom-call | flops 1140850688 | bytes 4194304 | tf_op jit(solution)/shard_map/pallas_call | solution.py:98
  36.6 0.1 all-to-all-done.1
  36.7 0.2 convert_reduce_fusion
  36.9 0.1 collective-permute-start
  37.0 1.2 %collective-permute-done = f32[2,3584]{1,0:T(2,128)S(1)} collective-permute-done((f32[2,3584]{1,0:T(2,128)S(1)}, f32[2,3584]{1,0:T(2,128)S(1)}, u32[]{:S(2)}, u32[]{:S(2)}) %collective-permute-start) | collective-permute-done | bytes 28704 | tf_op jit(solution)/shard_map/ppermute | solution.py:264
  38.1 0.6 %add_convert_fusion = bf16[2,3584]{1,0:T(2,128)(2,1)} fusion(f32[2,3584]{1,0:T(2,128)S(1)} %convert_reduce_fusion, f32[2,3584]{1,0:T(2,128)S(1)} %collective-permute-done), kind=kLoop, calls=%fused_computation.1 | loop fusion | flops 14336 | bytes 71680 | tf_op jit(solution)/shard_map/convert_element_type | solution.py:265
Async XLA Ops:
  2.2 15.2 %all-to-all-start = ((bf16[16,2,3712]{2,1,0:T(2,128)(2,1)}), bf16[16,2,3712]{2,1,0:T(2,128)(2,1)S(1)}, u32[]{:S(2)}, u32[]{:S(2)}) async-start(bf16[16,2,3712]{2,1,0:T(2,128)(2,1)} %shard_map.122), calls=%async_computation | async-start | bytes 475136 | tf_op jit(solution)/shard_map/all_to_all | solution.py:246
  25.5 11.2 %all-to-all-start.1 = ((bf16[16,2,3584]{2,1,0:T(2,128)(2,1)}), bf16[16,2,3584]{2,1,0:T(2,128)(2,1)S(1)}, u32[]{:S(2)}, u32[]{:S(2)}) async-start(bf16[16,2,3584]{2,1,0:T(2,128)(2,1)} %shard_map.124), calls=%async_computation.1 | async-start | bytes 458752 | tf_op jit(solution)/shard_map/all_to_all | solution.py:246
  36.9 1.3 %collective-permute-start = (f32[2,3584]{1,0:T(2,128)S(1)}, f32[2,3584]{1,0:T(2,128)S(1)}, u32[]{:S(2)}, u32[]{:S(2)}) collective-permute-start(f32[2,3584]{1,0:T(2,128)S(1)} %convert_reduce_fusion), channel_id=1, source_target_pairs={{0,1},{1,0},{2,3},{3,2},{4,5},{5,4},{6,7},{7,6},{8,9},{9,8},{10,11... | collective-permute-start | bytes 86024 | tf_op jit(solution)/shard_map/ppermute | solution.py:264

commit v5 on v4

--- a/solution.py
+++ b/solution.py
@@ -27,7 +27,7 @@
     rope_width = rope_keys.shape[0]
     heads_here = q_latent.shape[1] // latent_width // parts
     rows = heads_here * requests
-    block = min(512, total)
+    block = min(1024, total)
     wide, thin = heads_here * latent_width, heads_here * rope_width
     ff = early[0].shape[1] if early else 0
     chunks = [(k, block) for k in range(0, total, block)]
@@ -79,12 +79,12 @@
                 highest = jnp.maximum(highest, masked[:, :, j : j + LANES])
         scale = score_scale * LOG2E
         top = jnp.max(highest, axis=2, keepdims=True).reshape(rows, 1) * scale
-        step = 64
+        step = min(rows, 256)
         for k in range(0, rows, step):
             own = slice(k, k + step)
             weights = jnp.exp2(scores[own, :] * scale - top[own])
-            shares = (weights * (1.0 / jnp.sum(weights, axis=1, keepdims=True))).astype(jnp.bfloat16)
-            result = jnp.dot(shares, latent_buf[...], preferred_element_type=jnp.float32)
+            whole = 1.0 / jnp.sum(weights, axis=1, keepdims=True)
+            result = jnp.dot(weights.astype(jnp.bfloat16), latent_buf[...], preferred_element_type=jnp.float32) * whole
             for j in range(0, step, requests):
                 h = (k + j) // requests
                 out_buf[:, h * latent_width : (h + 1) * latent_width] = result[j : j + requests].astype(jnp.bfloat16)

time: 39.2 us -> 39.2 us (level)
  waiting for transfers between devices: 2.48 us -> 4.38 us
  Pallas kernels: 20 us -> 18.1 us
    pallas_call x2, Pallas kernels: 10.4 us -> 8.51 us  [attend(): pl.pallas_call(kernel, out_shape=[pltpu.HBM(q_latent.shape, jnp.bfloat16)...]
    all_to_all x2, waiting for transfers between devices: 1.29 us -> 3.19 us  [swap(): lax.all_to_all(blocks, axes, split_axis=0, concat_axis=0, tiled=True, axi...]
  transfers between devices with their start and end apart: 3 -> 3, of which waited for: 3 -> 3; matrix products, arithmetic and copies ran while one was open for 0% -> 0% of each run, Pallas kernels for 27% -> 22%
where the time goes in v5:
time: 39.2 us; the launch traced here: 38.8 us
  Pallas kernels  18.1 us (46%)
  starting transfers between devices  14.8 us (38%)
  waiting for transfers between devices  4.38 us (11%)
  other arithmetic  0.81 us (2%)
  between operations  0.67 us (2%)
    all_to_all x2, starting transfers between devices, swap(): lax.all_to_all(blocks, axes, split_axis=0, concat_axis=0, tiled=True, axi...  14.7 us
    pallas_call x2, Pallas kernels, attend(): pl.pallas_call(kernel, out_shape=[pltpu.HBM(q_latent.shape, jnp.bfloat16)...  8.51 us
    pallas_call x1, Pallas kernels, experts(): pl.pallas_call(kernel, out_shape=pltpu.HBM(rows.shape[:2] + (width,), jnp...  8.11 us
    all_to_all x2, waiting for transfers between devices, swap(): lax.all_to_all(blocks, axes, split_axis=0, concat_axis=0, tiled=True, axi...  3.19 us
    pallas_call x1, Pallas kernels, pack(): pl.pallas_call(pack_kernel, out_shape=jax.ShapeDtypeStruct((copies, token...  1.52 us
    ppermute x1, waiting for transfers between devices, local(): other = lax.ppermute(local_sum, 'heads', [(0, 1), (1, 0)])  1.19 us
  transfers between devices with their start and end apart: 3, of which 3 were waited for; matrix products, arithmetic and copies ran while one was open for 0% of the time, Pallas kernels for 22%

profile of v5, /device:TPU:0, one launch (start us, length us, event | category | flops | bytes accessed | tf_op | source)
XLA Modules:
  0.0 38.8 jit_solution(15161172515978706599)
XLA Ops:
  0.6 1.5 %shard_map.122 = bf16[16,2,3712]{2,1,0:T(2,128)(2,1)} custom-call(bf16[2,3584]{1,0:T(2,128)(2,1)} %tokens_ref.1, s32[2,8]{1,0:T(2,128)} %routes_ref.1, bf16[2,8]{1,0:T(2,128)(2,1)} %gates_ref.1), custom_call_target="tpu_custom_call" | custom-call | tf_op jit(solution)/shard_map/pallas_call | solution.py:155
  2.2 8.8 %all-to-all-start = ((bf16[16,2,3712]{2,1,0:T(2,128)(2,1)}), bf16[16,2,3712]{2,1,0:T(2,128)(2,1)S(1)}, u32[]{:S(2)}, u32[]{:S(2)}) async-start(bf16[16,2,3712]{2,1,0:T(2,128)(2,1)} %shard_map.122), calls=%async_computation | async-start | bytes 475136 | tf_op jit(solution)/shard_map/all_to_all | solution.py:246
  11.0 4.3 %shard_map.123 = (bf16[8,32768]{1,0:T(8,128)(2,1)}, bf16[512,1024]{1,0:T(8,128)(2,1)S(1)}, bf16[512,1024]{1,0:T(8,128)(2,1)S(1)}, bf16[512,1024]{1,0:T(8,128)(2,1)S(1)}) custom-call(s32[1]{0:T(128)} %bitcast.1.share_ref, s32[1,8]{1,0:T(1,128)} %lengths_ref.3, bf16[8,32768]{1,0:T(8,128)(2,1)} %q_ref.3, bf16[8,4096]{1,0:T(8,128)(2,1)} %q_rope_ref.3, ...), custom_call_target="tpu_custom_call" | custom-call | flops 1140850688 | bytes 4194304 | tf_op jit(solution)/shard_map/pallas_call | solution.py:98
  15.2 2.1 %all-to-all-done.rows_ref = bf16[16,2,3712]{2,1,0:T(2,128)(2,1)S(1)} async-done(((bf16[16,2,3712]{2,1,0:T(2,128)(2,1)}), bf16[16,2,3712]{2,1,0:T(2,128)(2,1)S(1)}, u32[]{:S(2)}, u32[]{:S(2)}) %all-to-all-start) | async-done | bytes 237600 | tf_op jit(solution)/shard_map/all_to_all | solution.py:246
  17.4 8.1 %shard_map.124 = bf16[16,2,3584]{2,1,0:T(2,128)(2,1)} custom-call(s32[1]{0:T(128)} %bitcast.expert_ref, s32[1]{0:T(128)} %bitcast.1.share_ref, bf16[16,2,3712]{2,1,0:T(2,128)(2,1)S(1)} %all-to-all-done.rows_ref, bf16[3584,2048]{1,0:T(8,128)(2,1)} %gate_ref.1, bf16[3584,2048]{1,0:T(8,128)(2,1)} %up_ref.1, bf16[2048,3584]{1,0:T(8,128)(2,1)} %down_ref.1, ...), custom_call_target="tpu_custom_call" | custom-call | tf_op jit(solution)/shard_map/pallas_call | solution.py:212
  25.5 5.9 %all-to-all-start.1 = ((bf16[16,2,3584]{2,1,0:T(2,128)(2,1)}), bf16[16,2,3584]{2,1,0:T(2,128)(2,1)S(1)}, u32[]{:S(2)}, u32[]{:S(2)}) async-start(bf16[16,2,3584]{2,1,0:T(2,128)(2,1)} %shard_map.124), calls=%async_computation.1 | async-start | bytes 458752 | tf_op jit(solution)/shard_map/all_to_all | solution.py:246
  31.4 4.2 %shard_map.125 = bf16[8,32768]{1,0:T(8,128)(2,1)} custom-call(s32[1]{0:T(128)} %bitcast.1.share_ref, s32[1,8]{1,0:T(1,128)} %lengths_ref.3, bf16[8,32768]{1,0:T(8,128)(2,1)} %q_ref.3, bf16[8,4096]{1,0:T(8,128)(2,1)} %q_rope_ref.3, bf16[2048,512]{1,0:T(8,128)(2,1)} %latent_ref.3, bf16[64,2048]{1,0:T(8,128)(2,1)} %rope_ref.3, ...), custom_call_target="tpu_custom_call", output_to_operand_aliasing={{}: (6, {})} | custom-call | flops 1140850688 | bytes 4194304 | tf_op jit(solution)/shard_map/pallas_call | solution.py:98
  35.6 1.1 %all-to-all-done.1 = bf16[16,2,3584]{2,1,0:T(2,128)(2,1)S(1)} async-done(((bf16[16,2,3584]{2,1,0:T(2,128)(2,1)}), bf16[16,2,3584]{2,1,0:T(2,128)(2,1)S(1)}, u32[]{:S(2)}, u32[]{:S(2)}) %all-to-all-start.1) | async-done | bytes 229408 | tf_op jit(solution)/shard_map/all_to_all | solution.py:246
  36.7 0.2 convert_reduce_fusion
  36.9 0.1 collective-permute-start
  37.0 1.2 %collective-permute-done = f32[2,3584]{1,0:T(2,128)S(1)} collective-permute-done((f32[2,3584]{1,0:T(2,128)S(1)}, f32[2,3584]{1,0:T(2,128)S(1)}, u32[]{:S(2)}, u32[]{:S(2)}) %collective-permute-start) | collective-permute-done | bytes 28704 | tf_op jit(solution)/shard_map/ppermute | solution.py:264
  38.1 0.6 %add_convert_fusion = bf16[2,3584]{1,0:T(2,128)(2,1)} fusion(f32[2,3584]{1,0:T(2,128)S(1)} %convert_reduce_fusion, f32[2,3584]{1,0:T(2,128)S(1)} %collective-permute-done), kind=kLoop, calls=%fused_computation.1 | loop fusion | flops 14336 | bytes 71680 | tf_op jit(solution)/shard_map/convert_element_type | solution.py:265
Async XLA Ops:
  2.2 15.2 %all-to-all-start = ((bf16[16,2,3712]{2,1,0:T(2,128)(2,1)}), bf16[16,2,3712]{2,1,0:T(2,128)(2,1)S(1)}, u32[]{:S(2)}, u32[]{:S(2)}) async-start(bf16[16,2,3712]{2,1,0:T(2,128)(2,1)} %shard_map.122), calls=%async_computation | async-start | bytes 475136 | tf_op jit(solution)/shard_map/all_to_all | solution.py:246
  25.5 11.2 %all-to-all-start.1 = ((bf16[16,2,3584]{2,1,0:T(2,128)(2,1)}), bf16[16,2,3584]{2,1,0:T(2,128)(2,1)S(1)}, u32[]{:S(2)}, u32[]{:S(2)}) async-start(bf16[16,2,3584]{2,1,0:T(2,128)(2,1)} %shard_map.124), calls=%async_computation.1 | async-start | bytes 458752 | tf_op jit(solution)/shard_map/all_to_all | solution.py:246
  36.9 1.3 %collective-permute-start = (f32[2,3584]{1,0:T(2,128)S(1)}, f32[2,3584]{1,0:T(2,128)S(1)}, u32[]{:S(2)}, u32[]{:S(2)}) collective-permute-start(f32[2,3584]{1,0:T(2,128)S(1)} %convert_reduce_fusion), channel_id=1, source_target_pairs={{0,1},{1,0},{2,3},{3,2},{4,5},{5,4},{6,7},{7,6},{8,9},{9,8},{10,11... | collective-permute-start | bytes 86024 | tf_op jit(solution)/shard_map/ppermute | solution.py:264

commit v6 on v5

--- a/solution.py
+++ b/solution.py
@@ -170,7 +170,7 @@
 def experts(own_expert, share, shares, rows, w_gate, w_up, w_down, early):
     width = w_down.shape[1]
     ff = w_down.shape[0] // shares
-    thin, wide = cuts(width, 512), cuts(ff, 256)
+    thin, wide = cuts(width, 512), cuts(ff, 64)
 
     def kernel(expert_ref, share_ref, rows_ref, gate_ref, up_ref, down_ref, *refs):
         early_refs, (out_ref, gate_buf, up_buf, down_buf, out_buf, sems) = refs[: len(early)], refs[len(early) :]
@@ -232,9 +232,7 @@
     pool_count = lax.axis_size("pool")
     head_count = lax.axis_size("heads")
     slices = pool_count * head_count // EXPERTS
-    own_pool = lax.axis_index("pool")
-    own_expert = (own_pool * head_count + lax.axis_index("heads")) // slices
-
+    own_expert = (lax.axis_index("pool") * head_count + lax.axis_index("heads")) // slices
     group_count = lax.axis_size("groups")
     apart = w_down.shape[0] % (group_count * 256) == 0
     shares, axes = (group_count, ("groups", "pool")) if apart else (1, ("pool",))

time: 39.2 us -> 38.8 us (0.990)
  Pallas kernels: 18.1 us -> 17.7 us
    pallas_call x1, Pallas kernels: 8.11 us -> 7.69 us  [experts(): pl.pallas_call(kernel, out_shape=pltpu.HBM(rows.shape[:2] + (width,), jnp...]
where the time goes in v6:
time: 38.8 us; the launch traced here: 38.3 us
  Pallas kernels  17.7 us (46%)
  starting transfers between devices  14.8 us (38%)
  waiting for transfers between devices  4.4 us (11%)
  other arithmetic  0.81 us (2%)
  between operations  0.67 us (2%)
    all_to_all x2, starting transfers between devices, swap(): lax.all_to_all(blocks, axes, split_axis=0, concat_axis=0, tiled=True, axi...  14.7 us
    pallas_call x2, Pallas kernels, attend(): pl.pallas_call(kernel, out_shape=[pltpu.HBM(q_latent.shape, jnp.bfloat16)...  8.49 us
    pallas_call x1, Pallas kernels, experts(): pl.pallas_call(kernel, out_shape=pltpu.HBM(rows.shape[:2] + (width,), jnp...  7.69 us
    all_to_all x2, waiting for transfers between devices, swap(): lax.all_to_all(blocks, axes, split_axis=0, concat_axis=0, tiled=True, axi...  3.21 us
    pallas_call x1, Pallas kernels, pack(): pl.pallas_call(pack_kernel, out_shape=jax.ShapeDtypeStruct((copies, token...  1.52 us
    ppermute x1, waiting for transfers between devices, local(): other = lax.ppermute(local_sum, 'heads', [(0, 1), (1, 0)])  1.19 us
  transfers between devices with their start and end apart: 3, of which 3 were waited for; matrix products, arithmetic and copies ran while one was open for 0% of the time, Pallas kernels for 22%

profile of v6, /device:TPU:0, one launch (start us, length us, event | category | flops | bytes accessed | tf_op | source)
XLA Modules:
  0.0 38.3 jit_solution(1696010113811088572)
XLA Ops:
  0.6 1.5 %shard_map.122 = bf16[16,2,3712]{2,1,0:T(2,128)(2,1)} custom-call(bf16[2,3584]{1,0:T(2,128)(2,1)} %tokens_ref.1, s32[2,8]{1,0:T(2,128)} %routes_ref.1, bf16[2,8]{1,0:T(2,128)(2,1)} %gates_ref.1), custom_call_target="tpu_custom_call" | custom-call | tf_op jit(solution)/shard_map/pallas_call | solution.py:155
  2.2 8.8 %all-to-all-start = ((bf16[16,2,3712]{2,1,0:T(2,128)(2,1)}), bf16[16,2,3712]{2,1,0:T(2,128)(2,1)S(1)}, u32[]{:S(2)}, u32[]{:S(2)}) async-start(bf16[16,2,3712]{2,1,0:T(2,128)(2,1)} %shard_map.122), calls=%async_computation | async-start | bytes 475136 | tf_op jit(solution)/shard_map/all_to_all | solution.py:244
  11.0 4.3 %shard_map.123 = (bf16[8,32768]{1,0:T(8,128)(2,1)}, bf16[512,1024]{1,0:T(8,128)(2,1)S(1)}, bf16[512,1024]{1,0:T(8,128)(2,1)S(1)}, bf16[512,1024]{1,0:T(8,128)(2,1)S(1)}) custom-call(s32[1]{0:T(128)} %bitcast.1.share_ref, s32[1,8]{1,0:T(1,128)} %lengths_ref.3, bf16[8,32768]{1,0:T(8,128)(2,1)} %q_ref.3, bf16[8,4096]{1,0:T(8,128)(2,1)} %q_rope_ref.3, ...), custom_call_target="tpu_custom_call" | custom-call | flops 1140850688 | bytes 4194304 | tf_op jit(solution)/shard_map/pallas_call | solution.py:98
  15.2 2.1 %all-to-all-done.rows_ref = bf16[16,2,3712]{2,1,0:T(2,128)(2,1)S(1)} async-done(((bf16[16,2,3712]{2,1,0:T(2,128)(2,1)}), bf16[16,2,3712]{2,1,0:T(2,128)(2,1)S(1)}, u32[]{:S(2)}, u32[]{:S(2)}) %all-to-all-start) | async-done | bytes 237600 | tf_op jit(solution)/shard_map/all_to_all | solution.py:244
  17.4 7.7 %shard_map.124 = bf16[16,2,3584]{2,1,0:T(2,128)(2,1)} custom-call(s32[1]{0:T(128)} %bitcast.expert_ref, s32[1]{0:T(128)} %bitcast.1.share_ref, bf16[16,2,3712]{2,1,0:T(2,128)(2,1)S(1)} %all-to-all-done.rows_ref, bf16[3584,2048]{1,0:T(8,128)(2,1)} %gate_ref.1, bf16[3584,2048]{1,0:T(8,128)(2,1)} %up_ref.1, bf16[2048,3584]{1,0:T(8,128)(2,1)} %down_ref.1, ...), custom_call_target="tpu_custom_call" | custom-call | tf_op jit(solution)/shard_map/pallas_call | solution.py:212
  25.1 5.9 %all-to-all-start.1 = ((bf16[16,2,3584]{2,1,0:T(2,128)(2,1)}), bf16[16,2,3584]{2,1,0:T(2,128)(2,1)S(1)}, u32[]{:S(2)}, u32[]{:S(2)}) async-start(bf16[16,2,3584]{2,1,0:T(2,128)(2,1)} %shard_map.124), calls=%async_computation.1 | async-start | bytes 458752 | tf_op jit(solution)/shard_map/all_to_all | solution.py:244
  30.9 4.2 %shard_map.125 = bf16[8,32768]{1,0:T(8,128)(2,1)} custom-call(s32[1]{0:T(128)} %bitcast.1.share_ref, s32[1,8]{1,0:T(1,128)} %lengths_ref.3, bf16[8,32768]{1,0:T(8,128)(2,1)} %q_ref.3, bf16[8,4096]{1,0:T(8,128)(2,1)} %q_rope_ref.3, bf16[2048,512]{1,0:T(8,128)(2,1)} %latent_ref.3, bf16[64,2048]{1,0:T(8,128)(2,1)} %rope_ref.3, ...), custom_call_target="tpu_custom_call", output_to_operand_aliasing={{}: (6, {})} | custom-call | flops 1140850688 | bytes 4194304 | tf_op jit(solution)/shard_map/pallas_call | solution.py:98
  35.2 1.1 %all-to-all-done.1 = bf16[16,2,3584]{2,1,0:T(2,128)(2,1)S(1)} async-done(((bf16[16,2,3584]{2,1,0:T(2,128)(2,1)}), bf16[16,2,3584]{2,1,0:T(2,128)(2,1)S(1)}, u32[]{:S(2)}, u32[]{:S(2)}) %all-to-all-start.1) | async-done | bytes 229408 | tf_op jit(solution)/shard_map/all_to_all | solution.py:244
  36.3 0.2 convert_reduce_fusion
  36.5 0.1 collective-permute-start
  36.5 1.2 %collective-permute-done = f32[2,3584]{1,0:T(2,128)S(1)} collective-permute-done((f32[2,3584]{1,0:T(2,128)S(1)}, f32[2,3584]{1,0:T(2,128)S(1)}, u32[]{:S(2)}, u32[]{:S(2)}) %collective-permute-start) | collective-permute-done | bytes 28704 | tf_op jit(solution)/shard_map/ppermute | solution.py:262
  37.7 0.6 %add_convert_fusion = bf16[2,3584]{1,0:T(2,128)(2,1)} fusion(f32[2,3584]{1,0:T(2,128)S(1)} %convert_reduce_fusion, f32[2,3584]{1,0:T(2,128)S(1)} %collective-permute-done), kind=kLoop, calls=%fused_computation.1 | loop fusion | flops 14336 | bytes 71680 | tf_op jit(solution)/shard_map/convert_element_type | solution.py:263
Async XLA Ops:
  2.2 15.2 %all-to-all-start = ((bf16[16,2,3712]{2,1,0:T(2,128)(2,1)}), bf16[16,2,3712]{2,1,0:T(2,128)(2,1)S(1)}, u32[]{:S(2)}, u32[]{:S(2)}) async-start(bf16[16,2,3712]{2,1,0:T(2,128)(2,1)} %shard_map.122), calls=%async_computation | async-start | bytes 475136 | tf_op jit(solution)/shard_map/all_to_all | solution.py:244
  25.1 11.2 %all-to-all-start.1 = ((bf16[16,2,3584]{2,1,0:T(2,128)(2,1)}), bf16[16,2,3584]{2,1,0:T(2,128)(2,1)S(1)}, u32[]{:S(2)}, u32[]{:S(2)}) async-start(bf16[16,2,3584]{2,1,0:T(2,128)(2,1)} %shard_map.124), calls=%async_computation.1 | async-start | bytes 458752 | tf_op jit(solution)/shard_map/all_to_all | solution.py:244
  36.5 1.3 %collective-permute-start = (f32[2,3584]{1,0:T(2,128)S(1)}, f32[2,3584]{1,0:T(2,128)S(1)}, u32[]{:S(2)}, u32[]{:S(2)}) collective-permute-start(f32[2,3584]{1,0:T(2,128)S(1)} %convert_reduce_fusion), channel_id=1, source_target_pairs={{0,1},{1,0},{2,3},{3,2},{4,5},{5,4},{6,7},{7,6},{8,9},{9,8},{10,11... | collective-permute-start | bytes 86024 | tf_op jit(solution)/shard_map/ppermute | solution.py:262

commit v7 on v6

--- a/solution.py
+++ b/solution.py
@@ -238,7 +238,9 @@
     shares, axes = (group_count, ("groups", "pool")) if apart else (1, ("pool",))
     peers = pool_count * shares
     middle = peers * 3 // 4
-    order = [middle] + [i for i in reversed(range(peers)) if i != middle]
+    order = [(middle + (peers // 2 + 1) * i) % peers for i in range(peers)]
+    if len(set(order)) < peers:
+        order = list(range(peers))
 
     def swap(blocks):
         return lax.all_to_all(blocks, axes, split_axis=0, concat_axis=0, tiled=True, axis_index_groups=[order])

time: 38.8 us -> 38.5 us (level)
  starting transfers between devices: 14.8 us -> 14 us
  waiting for transfers between devices: 4.4 us -> 4.88 us
    all_to_all x2, starting transfers between devices: 14.7 us -> 13.9 us  [swap(): lax.all_to_all(blocks, axes, split_axis=0, concat_axis=0, tiled=True, axi...]
    all_to_all x2, waiting for transfers between devices: 3.21 us -> 3.69 us  [swap(): lax.all_to_all(blocks, axes, split_axis=0, concat_axis=0, tiled=True, axi...]
where the time goes in v7:
time: 38.5 us; the launch traced here: 38.1 us
  Pallas kernels  17.7 us (46%)
  starting transfers between devices  14 us (36%)
  waiting for transfers between devices  4.88 us (13%)
  other arithmetic  0.81 us (2%)
  between operations  0.67 us (2%)
    all_to_all x2, starting transfers between devices, swap(): lax.all_to_all(blocks, axes, split_axis=0, concat_axis=0, tiled=True, axi...  13.9 us
    pallas_call x2, Pallas kernels, attend(): pl.pallas_call(kernel, out_shape=[pltpu.HBM(q_latent.shape, jnp.bfloat16)...  8.5 us
    pallas_call x1, Pallas kernels, experts(): pl.pallas_call(kernel, out_shape=pltpu.HBM(rows.shape[:2] + (width,), jnp...  7.69 us
    all_to_all x2, waiting for transfers between devices, swap(): lax.all_to_all(blocks, axes, split_axis=0, concat_axis=0, tiled=True, axi...  3.69 us
    pallas_call x1, Pallas kernels, pack(): pl.pallas_call(pack_kernel, out_shape=jax.ShapeDtypeStruct((copies, token...  1.52 us
    ppermute x1, waiting for transfers between devices, local(): other = lax.ppermute(local_sum, 'heads', [(0, 1), (1, 0)])  1.19 us
  transfers between devices with their start and end apart: 3, of which 3 were waited for; matrix products, arithmetic and copies ran while one was open for 0% of the time, Pallas kernels for 22%

profile of v7, /device:TPU:0, one launch (start us, length us, event | category | flops | bytes accessed | tf_op | source)
XLA Modules:
  0.0 38.1 jit_solution(15729948899564350548)
XLA Ops:
  0.6 1.5 %shard_map.122 = bf16[16,2,3712]{2,1,0:T(2,128)(2,1)} custom-call(bf16[2,3584]{1,0:T(2,128)(2,1)} %tokens_ref.1, s32[2,8]{1,0:T(2,128)} %routes_ref.1, bf16[2,8]{1,0:T(2,128)(2,1)} %gates_ref.1), custom_call_target="tpu_custom_call" | custom-call | tf_op jit(solution)/shard_map/pallas_call | solution.py:155
  2.2 8.8 %all-to-all-start = ((bf16[16,2,3712]{2,1,0:T(2,128)(2,1)}), bf16[16,2,3712]{2,1,0:T(2,128)(2,1)S(1)}, u32[]{:S(2)}, u32[]{:S(2)}) async-start(bf16[16,2,3712]{2,1,0:T(2,128)(2,1)} %shard_map.122), calls=%async_computation | async-start | bytes 475136 | tf_op jit(solution)/shard_map/all_to_all | solution.py:246
  11.0 4.3 %shard_map.123 = (bf16[8,32768]{1,0:T(8,128)(2,1)}, bf16[512,1024]{1,0:T(8,128)(2,1)S(1)}, bf16[512,1024]{1,0:T(8,128)(2,1)S(1)}, bf16[512,1024]{1,0:T(8,128)(2,1)S(1)}) custom-call(s32[1]{0:T(128)} %bitcast.1.share_ref, s32[1,8]{1,0:T(1,128)} %lengths_ref.3, bf16[8,32768]{1,0:T(8,128)(2,1)} %q_ref.3, bf16[8,4096]{1,0:T(8,128)(2,1)} %q_rope_ref.3, ...), custom_call_target="tpu_custom_call" | custom-call | flops 1140850688 | bytes 4194304 | tf_op jit(solution)/shard_map/pallas_call | solution.py:98
  15.2 2.5 %all-to-all-done.rows_ref = bf16[16,2,3712]{2,1,0:T(2,128)(2,1)S(1)} async-done(((bf16[16,2,3712]{2,1,0:T(2,128)(2,1)}), bf16[16,2,3712]{2,1,0:T(2,128)(2,1)S(1)}, u32[]{:S(2)}, u32[]{:S(2)}) %all-to-all-start) | async-done | bytes 237600 | tf_op jit(solution)/shard_map/all_to_all | solution.py:246
  17.7 7.7 %shard_map.124 = bf16[16,2,3584]{2,1,0:T(2,128)(2,1)} custom-call(s32[1]{0:T(128)} %bitcast.expert_ref, s32[1]{0:T(128)} %bitcast.1.share_ref, bf16[16,2,3712]{2,1,0:T(2,128)(2,1)S(1)} %all-to-all-done.rows_ref, bf16[3584,2048]{1,0:T(8,128)(2,1)} %gate_ref.1, bf16[3584,2048]{1,0:T(8,128)(2,1)} %up_ref.1, bf16[2048,3584]{1,0:T(8,128)(2,1)} %down_ref.1, ...), custom_call_target="tpu_custom_call" | custom-call | tf_op jit(solution)/shard_map/pallas_call | solution.py:212
  25.4 5.1 %all-to-all-start.1 = ((bf16[16,2,3584]{2,1,0:T(2,128)(2,1)}), bf16[16,2,3584]{2,1,0:T(2,128)(2,1)S(1)}, u32[]{:S(2)}, u32[]{:S(2)}) async-start(bf16[16,2,3584]{2,1,0:T(2,128)(2,1)} %shard_map.124), calls=%async_computation.1 | async-start | bytes 458752 | tf_op jit(solution)/shard_map/all_to_all | solution.py:246
  30.5 4.2 %shard_map.125 = bf16[8,32768]{1,0:T(8,128)(2,1)} custom-call(s32[1]{0:T(128)} %bitcast.1.share_ref, s32[1,8]{1,0:T(1,128)} %lengths_ref.3, bf16[8,32768]{1,0:T(8,128)(2,1)} %q_ref.3, bf16[8,4096]{1,0:T(8,128)(2,1)} %q_rope_ref.3, bf16[2048,512]{1,0:T(8,128)(2,1)} %latent_ref.3, bf16[64,2048]{1,0:T(8,128)(2,1)} %rope_ref.3, ...), custom_call_target="tpu_custom_call", output_to_operand_aliasing={{}: (6, {})} | custom-call | flops 1140850688 | bytes 4194304 | tf_op jit(solution)/shard_map/pallas_call | solution.py:98
  34.7 1.2 %all-to-all-done.1 = bf16[16,2,3584]{2,1,0:T(2,128)(2,1)S(1)} async-done(((bf16[16,2,3584]{2,1,0:T(2,128)(2,1)}), bf16[16,2,3584]{2,1,0:T(2,128)(2,1)S(1)}, u32[]{:S(2)}, u32[]{:S(2)}) %all-to-all-start.1) | async-done | bytes 229408 | tf_op jit(solution)/shard_map/all_to_all | solution.py:246
  36.0 0.2 convert_reduce_fusion
  36.2 0.1 collective-permute-start
  36.3 1.2 %collective-permute-done = f32[2,3584]{1,0:T(2,128)S(1)} collective-permute-done((f32[2,3584]{1,0:T(2,128)S(1)}, f32[2,3584]{1,0:T(2,128)S(1)}, u32[]{:S(2)}, u32[]{:S(2)}) %collective-permute-start) | collective-permute-done | bytes 28704 | tf_op jit(solution)/shard_map/ppermute | solution.py:264
  37.4 0.6 %add_convert_fusion = bf16[2,3584]{1,0:T(2,128)(2,1)} fusion(f32[2,3584]{1,0:T(2,128)S(1)} %convert_reduce_fusion, f32[2,3584]{1,0:T(2,128)S(1)} %collective-permute-done), kind=kLoop, calls=%fused_computation.1 | loop fusion | flops 14336 | bytes 71680 | tf_op jit(solution)/shard_map/convert_element_type | solution.py:265
Async XLA Ops:
  2.2 15.5 %all-to-all-start = ((bf16[16,2,3712]{2,1,0:T(2,128)(2,1)}), bf16[16,2,3712]{2,1,0:T(2,128)(2,1)S(1)}, u32[]{:S(2)}, u32[]{:S(2)}) async-start(bf16[16,2,3712]{2,1,0:T(2,128)(2,1)} %shard_map.122), calls=%async_computation | async-start | bytes 475136 | tf_op jit(solution)/shard_map/all_to_all | solution.py:246
  25.4 10.6 %all-to-all-start.1 = ((bf16[16,2,3584]{2,1,0:T(2,128)(2,1)}), bf16[16,2,3584]{2,1,0:T(2,128)(2,1)S(1)}, u32[]{:S(2)}, u32[]{:S(2)}) async-start(bf16[16,2,3584]{2,1,0:T(2,128)(2,1)} %shard_map.124), calls=%async_computation.1 | async-start | bytes 458752 | tf_op jit(solution)/shard_map/all_to_all | solution.py:246
  36.2 1.3 %collective-permute-start = (f32[2,3584]{1,0:T(2,128)S(1)}, f32[2,3584]{1,0:T(2,128)S(1)}, u32[]{:S(2)}, u32[]{:S(2)}) collective-permute-start(f32[2,3584]{1,0:T(2,128)S(1)} %convert_reduce_fusion), channel_id=1, source_target_pairs={{0,1},{1,0},{2,3},{3,2},{4,5},{5,4},{6,7},{7,6},{8,9},{9,8},{10,11... | collective-permute-start | bytes 86024 | tf_op jit(solution)/shard_map/ppermute | solution.py:264
